TPU v7x, 768 devices: a whole 4x8x12 slice. The times are simulated.
768 devices in a mesh: dp: 32 (over x_hi, y, core), tensor: 24 (over x_lo, z).
Axes of the slice: x: 4 (x_hi: 2, x_lo: 2; x = x_hi * 2 + x_lo), y: 8, z: 12, core: 2. Of those that a mesh axis runs over, the one named last changes fastest.
Arguments:
- tokens: bfloat16 [4608, 6144], P(('dp', 'tensor')), may hold values from -24 to 24
- norm_gain: float32 [6144], replicated, may hold values from 0.5 to 2
- proj_weight: bfloat16 [6144, 6144], P(None, 'tensor'), may hold values from -0.078125 to 0.078125
- cotangent: bfloat16 [4608, 6144], P('dp', 'tensor'), may hold values from -6 to 6
Outputs:
- projected: bfloat16 [4608, 6144], P('dp', 'tensor')
- input_grad: bfloat16 [4608, 6144], P(('dp', 'tensor'))
- weight_grad: float32 [6144, 6144], P('dp', 'tensor')
- gain_grad: float32 [6144], replicated
All inputs are finite; a program needn't handle non-finite values.
Results may differ from a plain program's by a relative error of at most 0.024.
Values may be sent and summed in bfloat16 or wider, within the bound.
No kernel may reach another device: no remote copies, remote signals or barrier semaphores. Data moves between devices by JAX's collectives and lax.ppermute only.
A program may use at most 32 MiB of HBM per device.

v0:
```python
import jax
import jax.numpy as jnp
from jax import lax
from jax.sharding import PartitionSpec as P


def normalize(tokens, norm_gain):
    values = tokens.astype(jnp.float32)
    inverse = lax.rsqrt(jnp.mean(values * values, axis=-1, keepdims=True) + 1e-05)
    unit_rows = values * inverse
    return (inverse, unit_rows, unit_rows * norm_gain)


def quantize(normed):
    blocks = normed.reshape(normed.shape[0], normed.shape[1] // 128, 128)
    scales = (jnp.max(jnp.abs(blocks), axis=-1) + 1e-06) / 448.0
    payload = (blocks / scales[..., None]).astype(jnp.bfloat16)
    return (payload, scales)


def restore(payload, scales, features):
    return (
        (payload.astype(jnp.float32) * scales[..., None]).reshape(-1, features).astype(jnp.bfloat16)
    )


def body(tokens, norm_gain, proj_weight, cotangent):
    features = tokens.shape[1]
    inverse, unit_rows, normed = normalize(tokens, norm_gain)
    payload, scales = quantize(normed)
    got_payload, got_scales = (
        lax.all_gather(payload, "tensor", axis=0, tiled=True),
        lax.all_gather(scales.astype(jnp.bfloat16), "tensor", axis=0, tiled=True).astype(
            scales.dtype
        ),
    )
    restored = restore(got_payload, got_scales, features)
    projected = jnp.dot(restored, proj_weight, preferred_element_type=jnp.float32).astype(
        jnp.bfloat16
    )
    sliced = cotangent
    normed_grad = lax.psum_scatter(
        lax.dot_general(
            sliced, proj_weight, (((1,), (1,)), ((), ())), preferred_element_type=jnp.float32
        ).astype(jnp.bfloat16),
        "tensor",
        scatter_dimension=0,
        tiled=True,
    ).astype(jnp.float32)
    sliced = restored
    weight_grad = lax.psum_scatter(
        lax.dot_general(
            sliced, cotangent, (((0,), (0,)), ((), ())), preferred_element_type=jnp.float32
        ).astype(jnp.bfloat16),
        "dp",
        scatter_dimension=0,
        tiled=True,
    ).astype(jnp.float32)
    gain_part = jnp.sum(normed_grad * unit_rows, axis=0)
    gain_grad = lax.psum(gain_part, ("dp", "tensor"))
    scaled = normed_grad * norm_gain
    input_grad = (
        inverse * (scaled - unit_rows * jnp.mean(scaled * unit_rows, axis=-1, keepdims=True))
    ).astype(jnp.bfloat16)
    return (projected, input_grad, weight_grad, gain_grad)


def solution(mesh):
    placed = (P(("dp", "tensor"), None), P(), P(None, "tensor"), P("dp", "tensor"))
    return jax.shard_map(
        body,
        mesh=mesh,
        in_specs=placed,
        out_specs=(P("dp", "tensor"), P(("dp", "tensor"), None), P("dp", "tensor"), P()),
        check_vma=False,
    )
```

profile of v0, /device:TPU:16, one launch (start us, length us, event | category | flops | bytes accessed | tf_op | source)
XLA Modules:
  0.0 403.5 jit_solution(15216290533295726563)
XLA Ops:
  7.2 0.0 copy-start
  7.2 0.0 all-gather.3.cloned.1.call-start
  7.2 1.8 copy-done
  9.1 3.3 convolution_convert_fusion.1
  12.4 72.5 %fusion = bf16[8,6144]{1,0:T(8,128)(2,1)S(1)} fusion(bf16[144,6144]{1,0:T(8,128)(2,1)} %convolution_convert_fusion.1), kind=kCustom, calls=%all-reduce-scatter | all-reduce-scatter fusion | flops 1179649 | bytes 1871872
  84.8 3.0 collective-permute-start.4
  87.8 1.9 collective-permute-start.3
  89.8 12.6 %collective-permute-start.2 = (bf16[8,6144]{1,0:T(8,128)(2,1)S(1)}, bf16[8,6144]{1,0:T(8,128)(2,1)}, u32[]{:S(2)}, u32[]{:S(2)}) collective-permute-start(bf16[8,6144]{1,0:T(8,128)(2,1)S(1)} %fusion), channel_id=1, source_target_pairs={{0,3},{1,4},{2,5},{3,6},{4,7},{5,8},{6,9},{7,10},{8,11},{9,12},{10... | collective-permute-start | bytes 294920
  102.4 1.9 collective-permute-start.1
  104.4 2.8 collective-permute-start.5
  107.2 0.2 fusion.17
  107.4 7.4 %collective-permute-done.5 = bf16[6,6144]{1,0:T(8,128)(2,1)S(1)} collective-permute-done((bf16[6,6144]{1,0:T(8,128)(2,1)S(1)}, bf16[6,6144]{1,0:T(8,128)(2,1)S(1)}, u32[]{:S(2)}, u32[]{:S(2)}) %collective-permute-start.5) | collective-permute-done | bytes 73760
  114.8 0.6 copy-done.4
  115.4 1.9 collective-permute-start
  117.4 1.3 dynamic-slice.4
  119.4 19.3 %concatenate = bf16[54,6144]{1,0:T(8,128)(2,1)} concatenate(bf16[6,6144]{1,0:T(8,128)(2,1)} %copy-done.4, bf16[8,6144]{1,0:T(8,128)(2,1)S(1)} %collective-permute-done.4, bf16[8,6144]{1,0:T(8,128)(2,1)} %collective-permute-done.3, bf16[8,6144]{1,0:T(8,128)(2,1)} %collective-permute-done.2, bf16[8,6144]{1,0:T(8,128)(2,1)} %collective-permute-done.1, ...), dimensions={0} | concatenate | bytes 1327104
  138.7 1.2 fusion.18
  139.9 1.7 fusion.14
  141.7 0.1 fusion.19
  141.8 0.7 fusion.20
  142.5 0.0 all-gather.3.cloned.1.call-update
  142.5 0.0 reduce-scatter.4.cloned.1.call-start
  142.6 50.2 %all-gather = bf16[24,6,48]{2,1,0:T(8,128)(2,1)S(1)} all-gather(bf16[1,6,48]{2,1,0:T(8,128)(2,1)S(1)} %get-tuple-element.8), channel_id=1, replica_groups=mesh['dp'=32,'tensor'=24] {'tensor'}, dimensions={0}, use_global_device_ids=true | all-gather | bytes 14400 | tf_op jit(solution)/shard_map/all_gather | solution.py:33
  192.8 61.8 %all-gather.3.cloned.1.call-done = bf16[144,48,128]{2,1,0:T(8,128)(2,1)} async-done(((bf16[6,48,128]{2,1,0:T(8,128)(2,1)}), bf16[144,48,128]{2,1,0:T(8,128)(2,1)}) %all-gather.3.cloned.1.call-update) | async-done | bytes 1769488 | tf_op jit(solution)/shard_map/all_gather | solution.py:32
  254.6 2.2 multiply_convert_fusion
  256.9 1.2 copy-done.1
  258.1 2.7 convolution_convert_fusion
  260.9 0.0 reduce-scatter.4.cloned.1.call-update
  260.9 101.5 %psum.7 = f32[6144]{0:T(1024)} all-reduce(f32[6144]{0:T(1024)S(1)} %get-tuple-element.4), channel_id=1, replica_groups=mesh['dp'=32,'tensor'=24] {'dp','tensor'}, use_global_device_ids=true, to_apply=%region_6.0 | all-reduce | flops 6144 | bytes 49152 | tf_op jit(solution)/shard_map/psum | solution.py:60
  362.4 2.7 fusion.6
  365.1 30.0 %reduce-scatter.4.cloned.1.call-done = bf16[192,256]{1,0:T(8,128)(2,1)} async-done(((bf16[6144,256]{1,0:T(8,128)(2,1)}), bf16[192,256]{1,0:T(8,128)(2,1)}) %reduce-scatter.4.cloned.1.call-update) | async-done | bytes 98320 | tf_op jit(solution)/shard_map/reduce_scatter | solution.py:51
  395.1 1.6 convert_element_type.51
  (18 shorter events, 0.1 us)
Async XLA Ops:
  7.2 1.9 copy-start
  7.2 100.0 %copy-start.2 = (bf16[6,6144]{1,0:T(8,128)(2,1)S(1)}, bf16[6,6144]{1,0:T(8,128)(2,1)}, u32[]{:S(2)}) copy-start(bf16[6,6144]{1,0:T(8,128)(2,1)} %param.4) | copy-start | bytes 221188
  7.2 247.4 %all-gather.3.cloned.1.call-start = ((), (), s32[]{:S(2)}) async-start(), calls=%async_computation.1 | async-start | bytes 1843200 | tf_op jit(solution)/shard_map/all_gather | solution.py:32
  12.4 126.3 %copy-start.3 = (f32[6144]{0:T(1024)S(1)}, f32[6144]{0:T(1024)}, u32[]{:S(2)}) copy-start(f32[6144]{0:T(1024)} %param.5) | copy-start | bytes 73732
  84.8 34.5 %collective-permute-start.4 = (bf16[8,6144]{1,0:T(8,128)(2,1)S(1)}, bf16[8,6144]{1,0:T(8,128)(2,1)S(1)}, u32[]{:S(2)}, u32[]{:S(2)}) collective-permute-start(bf16[8,6144]{1,0:T(8,128)(2,1)S(1)} %fusion), channel_id=1, source_target_pairs={{0,5},{1,6},{2,7},{3,8},{4,9},{5,10},{6,11},{7,12},{8,13},{9,14},{... | collective-permute-start | bytes 294920
  87.8 31.5 %collective-permute-start.3 = (bf16[8,6144]{1,0:T(8,128)(2,1)S(1)}, bf16[8,6144]{1,0:T(8,128)(2,1)}, u32[]{:S(2)}, u32[]{:S(2)}) collective-permute-start(bf16[8,6144]{1,0:T(8,128)(2,1)S(1)} %fusion), channel_id=1, source_target_pairs={{0,4},{1,5},{2,6},{3,7},{4,8},{5,9},{6,10},{7,11},{8,12},{9,13},{1... | collective-permute-start | bytes 294920
  89.8 29.5 %collective-permute-start.2 = (bf16[8,6144]{1,0:T(8,128)(2,1)S(1)}, bf16[8,6144]{1,0:T(8,128)(2,1)}, u32[]{:S(2)}, u32[]{:S(2)}) collective-permute-start(bf16[8,6144]{1,0:T(8,128)(2,1)S(1)} %fusion), channel_id=1, source_target_pairs={{0,3},{1,4},{2,5},{3,6},{4,7},{5,8},{6,9},{7,10},{8,11},{9,12},{10... | collective-permute-start | bytes 294920
  102.4 16.9 %collective-permute-start.1 = (bf16[8,6144]{1,0:T(8,128)(2,1)S(1)}, bf16[8,6144]{1,0:T(8,128)(2,1)}, u32[]{:S(2)}, u32[]{:S(2)}) collective-permute-start(bf16[8,6144]{1,0:T(8,128)(2,1)S(1)} %fusion), channel_id=1, source_target_pairs={{0,2},{1,3},{2,4},{3,5},{4,6},{5,7},{6,8},{7,9},{8,10},{9,11},{10,... | collective-permute-start | bytes 294920
  104.4 10.4 %collective-permute-start.5 = (bf16[6,6144]{1,0:T(8,128)(2,1)S(1)}, bf16[6,6144]{1,0:T(8,128)(2,1)S(1)}, u32[]{:S(2)}, u32[]{:S(2)}) collective-permute-start(bf16[6,6144]{1,0:T(8,128)(2,1)S(1)} %slice), channel_id=1, source_target_pairs={{0,6},{1,7},{2,8},{3,9},{4,10},{5,11},{6,12},{7,13},{8,14},{9,15},... | collective-permute-start | bytes 221192
  114.8 0.6 copy-start.4
  115.4 3.9 collective-permute-start
  139.9 118.2 %copy-start.5 = (bf16[144,256]{1,0:T(8,128)(2,1)S(1)}, bf16[144,256]{1,0:T(8,128)(2,1)}, u32[]{:S(2)}) copy-start(bf16[144,256]{1,0:T(8,128)(2,1)} %param.7) | copy-start | bytes 221188
  142.5 252.5 %reduce-scatter.4.cloned.1.call-start = ((), (), s32[]{:S(2)}) async-start(), calls=%async_computation.2 | async-start | bytes 3244032 | tf_op jit(solution)/shard_map/reduce_scatter | solution.py:51
  256.9 1.2 copy-start.1
Sparse Core Ops, SparseCore 0:
  142.7 111.9 all-gather.2
  261.0 134.0 reduce-scatter.3
where the time goes:
time: 405 us; the launch traced here: 404 us
  blocking collectives  224 us (55%)
  waiting for transfers between devices  99.3 us (25%)
  local copies, waits for them, and re-layouts  24.4 us (6%)
  starting transfers between devices  24.3 us (6%)
  between operations  14.8 us (4%)
  matrix products  8.78 us (2%)
  other arithmetic  7.79 us (2%)
    psum x1, blocking collectives, body(): gain_grad = lax.psum(gain_part, ('dp', 'tensor'))  102 us
    unnamed x1, blocking collectives  72.5 us
    all_gather x1, waiting for transfers between devices, body(): lax.all_gather(payload, 'tensor', axis=0, tiled=True)  61.8 us
    all_gather x1, blocking collectives, body(): lax.all_gather(scales.astype(jnp.bfloat16), 'tensor', axis=0, tiled=True)  50.2 us
    reduce_scatter x1, waiting for transfers between devices, body(): lax.psum_scatter(lax.dot_general(sliced, cotangent, (((0,), (0,)), ((), (...  30 us
    unnamed x15, local copies, waits for them, and re-layouts  24.3 us
    unnamed x6, starting transfers between devices  24.2 us
  transfers between devices with their start and end apart: 8, of which 3 were waited for; matrix products, arithmetic and copies ran while one was open for 1% of the time, Pallas kernels for 0%

commit v1 on v0

v1 whole, which is shorter than its diff:
```python
import jax
import jax.numpy as jnp
from jax import lax
from jax.experimental import pallas as pl
from jax.experimental.pallas import tpu as pltpu
from jax.sharding import Mesh, PartitionSpec as P

XH, Y, CORE, XL, Z = 2, 8, 2, 2, 12
AXES = ("xh", "y", "c", "xl", "z")
DP, TENSOR = ("xh", "y", "c"), ("xl", "z")
TOK, D, COLS = 6, 6144, 256
Q, FQ = 4, 1536
GROUP = TOK * XL * Z
ROWS = GROUP * Q
BLOCK = 384
NT = (((1,), (1,)), ((), ()))
TN = (((0,), (0,)), ((), ()))


def grad_kernel(cot_ref, w_ref, term_ref, comm_ref, wide):
    for q in range(Q):
        part = lax.dot_general(
            cot_ref[...],
            w_ref[q * FQ : (q + 1) * FQ, :],
            NT,
            preferred_element_type=jnp.float32,
        )
        term_ref[:, q * FQ : (q + 1) * FQ] = part.astype(jnp.bfloat16)
        for b in range(FQ // 128):
            wide[b, pl.ds(q, GROUP, stride=Q), :] = part[:, b * 128 : (b + 1) * 128]
    for b in range(FQ // 128):
        comm_ref[:, b * 128 : (b + 1) * 128] = wide[b].astype(jnp.bfloat16)


def grad_terms(cotangent, weight):
    vmem = pl.BlockSpec(memory_space=pltpu.VMEM)
    return pl.pallas_call(
        grad_kernel,
        out_shape=(
            jax.ShapeDtypeStruct((GROUP, D), jnp.bfloat16),
            jax.ShapeDtypeStruct((ROWS, FQ), jnp.bfloat16),
        ),
        in_specs=[vmem] * 2,
        out_specs=(vmem, vmem),
        scratch_shapes=[pltpu.VMEM((FQ // 128, ROWS, 128), jnp.float32)],
        compiler_params=pltpu.CompilerParams(vmem_limit_bytes=40 * 2**20),
        cost_estimate=pl.CostEstimate(
            flops=2 * GROUP * D * COLS, bytes_accessed=7 * 2**20, transcendentals=0
        ),
    )(cotangent, weight)


def main_kernel(
    side_ref, own_ref, other_ref, w_ref, cot_ref, gain_ref, term_ref,
    proj_ref, wgrad_ref, part_ref, wide,
):
    half = ROWS // 2
    mine = pl.multiple_of(side_ref[0] * half, half)
    theirs = pl.multiple_of((1 - side_ref[0]) * half, half)
    for b in range(FQ // 128):
        wide[b, pl.ds(mine, half), :] = own_ref[:, b * 128 : (b + 1) * 128].astype(jnp.float32)
        wide[b, pl.ds(theirs, half), :] = other_ref[:, b * 128 : (b + 1) * 128].astype(jnp.float32)
    squares = jnp.zeros((GROUP, 128), jnp.float32)
    for b in range(FQ // 128):
        for q in range(Q):
            values = wide[b, pl.ds(q, GROUP, stride=Q), :]
            squares += values * values
    inverse = lax.rsqrt(jnp.sum(squares, axis=1, keepdims=True) / D + 1e-05)
    total = jnp.zeros((GROUP, COLS), jnp.float32)
    for p in range(D // BLOCK):
        q, first = divmod(p * BLOCK, FQ)
        pieces = []
        for b in range(BLOCK // 128):
            at = p * BLOCK + b * 128
            unit = wide[first // 128 + b, pl.ds(q, GROUP, stride=Q), :] * inverse
            part_ref[:, at : at + 128] = jnp.sum(
                unit * term_ref[:, at : at + 128].astype(jnp.float32), axis=0, keepdims=True
            )
            normed = unit * gain_ref[:, at : at + 128]
            scale = (jnp.max(jnp.abs(normed), axis=1, keepdims=True) + 1e-06) / 448.0
            payload = (normed / scale).astype(jnp.bfloat16)
            pieces.append((payload.astype(jnp.float32) * scale).astype(jnp.bfloat16))
        restored = jnp.concatenate(pieces, axis=1)
        total += jnp.dot(
            restored, w_ref[p * BLOCK : (p + 1) * BLOCK, :], preferred_element_type=jnp.float32
        )
        product = lax.dot_general(
            restored, cot_ref[...], TN, preferred_element_type=jnp.float32
        ).astype(jnp.bfloat16)
        wgrad_ref[0, p] = product[: BLOCK // 2]
        wgrad_ref[1, p] = product[BLOCK // 2 :]
    proj_ref[...] = total.astype(jnp.bfloat16)


def main_products(side, own, other, weight, cotangent, gain, term):
    vmem = pl.BlockSpec(memory_space=pltpu.VMEM)
    return pl.pallas_call(
        main_kernel,
        out_shape=(
            jax.ShapeDtypeStruct((GROUP, COLS), jnp.bfloat16),
            jax.ShapeDtypeStruct((CORE, XH * Y, BLOCK // 2, COLS), jnp.bfloat16),
            jax.ShapeDtypeStruct((1, D), jnp.float32),
        ),
        in_specs=[pl.BlockSpec(memory_space=pltpu.SMEM)] + [vmem] * 6,
        out_specs=(vmem, vmem, vmem),
        scratch_shapes=[pltpu.VMEM((FQ // 128, ROWS, 128), jnp.float32)],
        compiler_params=pltpu.CompilerParams(vmem_limit_bytes=40 * 2**20),
        cost_estimate=pl.CostEstimate(
            flops=4 * GROUP * D * COLS, bytes_accessed=12 * 2**20, transcendentals=0
        ),
    )(side, own, other, weight, cotangent, gain, term)


def exchange(array, axes):
    return lax.all_to_all(array, axes, 0, 0, tiled=True)


def body(tokens, norm_gain, proj_weight, cotangent):
    term, comm = grad_terms(cotangent, proj_weight)
    grad_rows = lax.psum_scatter(comm, TENSOR, scatter_dimension=0, tiled=True)

    chunk = tokens.reshape(TOK * Q, FQ)
    own = lax.all_gather(chunk, "z", axis=0, tiled=True)
    other = lax.ppermute(own, "xl", [(0, 1), (1, 0)])
    side = lax.axis_index("xl").astype(jnp.int32).reshape(1)
    projected, wgrad, part = main_products(
        side, own, other, proj_weight, cotangent, norm_gain.reshape(1, D), term
    )

    wgrad = exchange(wgrad, "c").astype(jnp.float32)
    wgrad = (wgrad[0] + wgrad[1]).astype(jnp.bfloat16)
    wgrad = exchange(wgrad, ("xh", "y"))
    weight_grad = jnp.sum(wgrad.astype(jnp.float32), axis=0)

    slots = XL * Z
    part = exchange(part.reshape(slots, D // slots), TENSOR)
    part = jnp.sum(part, axis=0)
    part = exchange(jnp.broadcast_to(part, (XH * Y * CORE, D // slots)), DP)
    part = jnp.sum(part, axis=0)
    part = exchange(jnp.broadcast_to(part, (slots, D // slots)), TENSOR)
    gain_grad = part.reshape(D)

    values = tokens.astype(jnp.float32)
    inverse = lax.rsqrt(jnp.mean(values * values, axis=-1, keepdims=True) + 1e-05)
    unit_rows = values * inverse
    normed_grad = grad_rows.reshape(TOK, D).astype(jnp.float32)
    scaled = normed_grad * norm_gain
    input_grad = (
        inverse * (scaled - unit_rows * jnp.mean(scaled * unit_rows, axis=-1, keepdims=True))
    ).astype(jnp.bfloat16)
    return projected, input_grad, weight_grad, gain_grad


def solution(mesh):
    fine = Mesh(mesh.devices.reshape(XH, Y, CORE, XL, Z), AXES)
    return jax.shard_map(
        body,
        mesh=fine,
        in_specs=(P(DP + TENSOR, None), P(), P(None, TENSOR), P(DP, TENSOR)),
        out_specs=(P(DP, TENSOR), P(DP + TENSOR, None), P(DP, TENSOR), P()),
        check_vma=False,
    )
```

time: 405 us -> 195 us (0.48)
  the two profiles are of different devices: /device:TPU:16 before, /device:TPU:8 now
where the time goes in v1:
time: 195 us; the launch traced here: 194 us
  waiting for transfers between devices  69.7 us (36%)
  blocking collectives  55.4 us (28%)
  starting transfers between devices  26.5 us (14%)
  between operations  14.1 us (7%)
  local copies, waits for them, and re-layouts  11.2 us (6%)
  other arithmetic  10.1 us (5%)
  Pallas kernels  6.96 us (4%)
    all_to_all x4, waiting for transfers between devices, exchange(): return lax.all_to_all(array, axes, 0, 0, tiled=True)  51.3 us
    all_gather x1, blocking collectives, body(): own = lax.all_gather(chunk, 'z', axis=0, tiled=True)  41.3 us
    all_to_all x4, starting transfers between devices, exchange(): return lax.all_to_all(array, axes, 0, 0, tiled=True)  22.9 us
    ppermute x1, waiting for transfers between devices, body(): other = lax.ppermute(own, 'xl', [(0, 1), (1, 0)])  18.4 us
    all_to_all x1, blocking collectives, exchange(): return lax.all_to_all(array, axes, 0, 0, tiled=True)  14.1 us
    unnamed x21, local copies, waits for them, and re-layouts  8.96 us
    pallas_call x1, Pallas kernels, main_products(): pl.pallas_call(main_kernel, out_shape=(jax.ShapeDtypeStruct((GROUP, COLS)...  5.44 us
    convert_element_type x1, other arithmetic, body(): wgrad = (wgrad[0] + wgrad[1]).astype(jnp.bfloat16)  4.5 us
  transfers between devices with their start and end apart: 6, of which 5 were waited for; matrix products, arithmetic and copies ran while one was open for 6% of the time, Pallas kernels for 3%

profile of v1, /device:TPU:8, one launch (start us, length us, event | category | flops | bytes accessed | tf_op | source)
XLA Modules:
  0.0 194.0 jit_solution(13292326111919990701)
XLA Ops:
  7.2 1.9 copy-done
  9.1 0.9 copy-done.6
  10.0 1.5 shard_map.75
  11.5 1.2 copy-done.3
  12.7 1.2 copy-done.4
  14.0 0.1 reshape.52
  14.1 41.3 %all_gather.3.own_ref = bf16[288,1536]{1,0:T(8,128)(2,1)} all-gather(bf16[24,1536]{1,0:T(8,128)(2,1)S(1)} %reshape.52), channel_id=1, replica_groups=mesh['xh'=2,'y'=8,'c'=2,'xl'=2,'z'=12] {'z'}, dimensions={0}, use_global_device_ids=true | all-gather | bytes 958464 | tf_op jit(solution)/shard_map/all_gather | solution.py:123
  55.3 3.6 %collective-permute-start = (bf16[288,1536]{1,0:T(8,128)(2,1)}, bf16[288,1536]{1,0:T(8,128)(2,1)}, u32[]{:S(2)}, u32[]{:S(2)}) collective-permute-start(bf16[288,1536]{1,0:T(8,128)(2,1)} %all_gather.3.own_ref), channel_id=1, source_target_pairs={{0,12},{12,0},{1,13},{13,1},{2,14},{14,2},{3,15},{15,3},{4,16},{16... | collective-permute-start | bytes 2654216 | tf_op jit(solution)/shard_map/ppermute | solution.py:124
  59.0 18.4 %collective-permute-done.other_ref = bf16[288,1536]{1,0:T(8,128)(2,1)} collective-permute-done((bf16[288,1536]{1,0:T(8,128)(2,1)}, bf16[288,1536]{1,0:T(8,128)(2,1)}, u32[]{:S(2)}, u32[]{:S(2)}) %collective-permute-start) | collective-permute-done | bytes 884768 | tf_op jit(solution)/shard_map/ppermute | solution.py:124
  77.4 1.5 copy-done.5
  78.9 5.4 %shard_map.76 = (bf16[144,256]{1,0:T(8,128)(2,1)}, bf16[2,16,192,256]{3,2,1,0:T(8,128)(2,1)S(1)}, f32[1,6144]{1,0:T(1,128)S(1)}) custom-call(s32[1]{0:T(128)} %bitcast.side_ref, bf16[288,1536]{1,0:T(8,128)(2,1)} %all_gather.3.own_ref, bf16[288,1536]{1,0:T(8,128)(2,1)} %collective-permute-done.other_ref, bf16[6144,256]{1,0:T(8,128)(2,1)S(1)} %copy-done.1, ...), custom_call_target="tpu_custom_call" | custom-call | flops 905969664 | bytes 12582912 | tf_op jit(solution)/shard_map/pallas_call | solution.py:97
  84.3 1.6 copy-done.2
  86.0 14.1 %all_to_all.31 = f32[24,1,256]{2,1,0:T(1,128)S(1)} all-to-all(f32[24,1,256]{2,1,0:T(1,128)S(1)} %bitcast.7), channel_id=1, replica_groups=mesh['xh'=2,'y'=8,'c'=2,'xl'=2,'z'=12] {'xl','z'}, dimensions={0} | all-to-all | bytes 49152 | tf_op jit(solution)/shard_map/all_to_all | solution.py:115
  100.1 4.0 %all-to-all-start = ((bf16[2,16,192,256]{3,2,1,0:T(8,128)(2,1)}), bf16[2,16,192,256]{3,2,1,0:T(8,128)(2,1)S(1)}, u32[]{:S(2)}, u32[]{:S(2)}) async-start(bf16[2,16,192,256]{3,2,1,0:T(8,128)(2,1)} %copy-done.2), calls=%async_computation.1 | async-start | bytes 6291456 | tf_op jit(solution)/shard_map/all_to_all | solution.py:115
  104.1 3.6 %all-to-all-done = bf16[2,16,192,256]{3,2,1,0:T(8,128)(2,1)S(1)} async-done(((bf16[2,16,192,256]{3,2,1,0:T(8,128)(2,1)}), bf16[2,16,192,256]{3,2,1,0:T(8,128)(2,1)S(1)}, u32[]{:S(2)}, u32[]{:S(2)}) %all-to-all-start) | async-done | bytes 3145760 | tf_op jit(solution)/shard_map/all_to_all | solution.py:115
  107.6 0.6 broadcast_in_dim.4
  108.3 10.2 %all-to-all-start.3 = ((f32[32,1,256]{2,1,0:T(1,128)}), f32[32,1,256]{2,1,0:T(1,128)S(1)}, u32[]{:S(2)}, u32[]{:S(2)}) async-start(f32[32,1,256]{2,1,0:T(1,128)} %broadcast_in_dim.4), calls=%async_computation.4 | async-start | bytes 65536 | tf_op jit(solution)/shard_map/all_to_all | solution.py:115
  118.4 3.4 %convert_element_type.28 = f32[2,16,192,256]{3,2,1,0:T(8,128)} convert(bf16[2,16,192,256]{3,2,1,0:T(8,128)(2,1)S(1)} %all-to-all-done) | non-fusion elementwise | flops 1572864 | bytes 9437184 | tf_op jit(solution)/shard_map/convert_element_type | solution.py:130
  121.9 5.5 %all-to-all-done.3 = f32[32,1,256]{2,1,0:T(1,128)S(1)} async-done(((f32[32,1,256]{2,1,0:T(1,128)}), f32[32,1,256]{2,1,0:T(1,128)S(1)}, u32[]{:S(2)}, u32[]{:S(2)}) %all-to-all-start.3) | async-done | bytes 32800 | tf_op jit(solution)/shard_map/all_to_all | solution.py:115
  127.3 0.1 reduce_sum.49
  127.4 0.6 broadcast_in_dim.10
  128.0 3.8 %all-to-all-start.4 = ((f32[24,1,256]{2,1,0:T(1,128)}), f32[24,1,256]{2,1,0:T(1,128)S(1)}, u32[]{:S(2)}, u32[]{:S(2)}) async-start(f32[24,1,256]{2,1,0:T(1,128)} %broadcast_in_dim.10), calls=%async_computation.5 | async-start | bytes 49152 | tf_op jit(solution)/shard_map/all_to_all | solution.py:115
  131.9 4.5 %fusion.1 = bf16[16,192,256]{2,1,0:T(8,128)(2,1)} fusion(f32[2,16,192,256]{3,2,1,0:T(8,128)} %convert_element_type.28), kind=kLoop, calls=%fused_computation.3 | loop fusion | flops 1572864 | bytes 7864320 | tf_op jit(solution)/shard_map/convert_element_type | solution.py:131
  136.3 6.3 %all-to-all-done.4 = f32[24,1,256]{2,1,0:T(1,128)S(1)} async-done(((f32[24,1,256]{2,1,0:T(1,128)}), f32[24,1,256]{2,1,0:T(1,128)S(1)}, u32[]{:S(2)}, u32[]{:S(2)}) %all-to-all-start.4) | async-done | bytes 24608 | tf_op jit(solution)/shard_map/all_to_all | solution.py:115
  142.6 4.9 %all-to-all-start.1 = ((bf16[16,192,256]{2,1,0:T(8,128)(2,1)}), bf16[16,192,256]{2,1,0:T(8,128)(2,1)S(1)}, u32[]{:S(2)}, u32[]{:S(2)}) async-start(bf16[16,192,256]{2,1,0:T(8,128)(2,1)} %fusion.1), calls=%async_computation.2 | async-start | bytes 3145728 | tf_op jit(solution)/shard_map/all_to_all | solution.py:115
  147.5 0.2 fusion.8
  147.7 0.9 reshape.55
  148.7 0.2 fusion.4
  148.9 0.7 fusion.7
  149.7 36.0 %all-to-all-done.1 = bf16[16,192,256]{2,1,0:T(8,128)(2,1)S(1)} async-done(((bf16[16,192,256]{2,1,0:T(8,128)(2,1)}), bf16[16,192,256]{2,1,0:T(8,128)(2,1)S(1)}, u32[]{:S(2)}, u32[]{:S(2)}) %all-to-all-start.1) | async-done | bytes 1572896 | tf_op jit(solution)/shard_map/all_to_all | solution.py:115
  185.6 0.9 convert_reduce_fusion
  186.5 0.6 copy.14
  (20 shorter events, 0.2 us)
Async XLA Ops:
  7.2 140.6 %reduce-scatter.2.cloned.1.call-start = ((), (), s32[]{:S(2)}) async-start(), calls=%async_computation.6 | async-start | bytes 1843200 | tf_op jit(solution)/shard_map/reduce_scatter | solution.py:120
  7.2 1.9 copy-start
  9.1 0.9 copy-start.6
  10.0 4.0 %copy-start.9 = (bf16[6,6144]{1,0:T(8,128)(2,1)S(1)}, bf16[6,6144]{1,0:T(8,128)(2,1)}, u32[]{:S(2)}) copy-start(bf16[6,6144]{1,0:T(8,128)(2,1)} %param.4) | copy-start | bytes 221188
  10.0 67.4 %copy-start.1 = (bf16[6144,256]{1,0:T(8,128)(2,1)S(1)}, bf16[6144,256]{1,0:T(8,128)(2,1)}, u32[]{:S(2)}) copy-start(bf16[6144,256]{1,0:T(8,128)(2,1)} %w_ref.3) | copy-start | bytes 9437188
  10.0 67.4 %copy-start.7 = (bf16[144,256]{1,0:T(8,128)(2,1)S(1)}, bf16[144,256]{1,0:T(8,128)(2,1)}, u32[]{:S(2)}) copy-start(bf16[144,256]{1,0:T(8,128)(2,1)} %cot_ref.3) | copy-start | bytes 221188
  10.0 67.4 %copy-start.8 = (f32[6144]{0:T(1024)S(1)}, f32[6144]{0:T(1024)}, u32[]{:S(2)}) copy-start(f32[6144]{0:T(1024)} %param.5) | copy-start | bytes 73732
  11.5 1.2 copy-start.3
  12.7 1.2 copy-start.4
  55.3 22.0 %collective-permute-start = (bf16[288,1536]{1,0:T(8,128)(2,1)}, bf16[288,1536]{1,0:T(8,128)(2,1)}, u32[]{:S(2)}, u32[]{:S(2)}) collective-permute-start(bf16[288,1536]{1,0:T(8,128)(2,1)} %all_gather.3.own_ref), channel_id=1, source_target_pairs={{0,12},{12,0},{1,13},{13,1},{2,14},{14,2},{3,15},{15,3},{4,16},{16... | collective-permute-start | bytes 2654216 | tf_op jit(solution)/shard_map/ppermute | solution.py:124
  77.4 1.5 copy-start.5
  84.3 1.6 copy-start.2
  100.1 7.6 %all-to-all-start = ((bf16[2,16,192,256]{3,2,1,0:T(8,128)(2,1)}), bf16[2,16,192,256]{3,2,1,0:T(8,128)(2,1)S(1)}, u32[]{:S(2)}, u32[]{:S(2)}) async-start(bf16[2,16,192,256]{3,2,1,0:T(8,128)(2,1)} %copy-done.2), calls=%async_computation.1 | async-start | bytes 6291456 | tf_op jit(solution)/shard_map/all_to_all | solution.py:115
  108.3 19.1 %all-to-all-start.3 = ((f32[32,1,256]{2,1,0:T(1,128)}), f32[32,1,256]{2,1,0:T(1,128)S(1)}, u32[]{:S(2)}, u32[]{:S(2)}) async-start(f32[32,1,256]{2,1,0:T(1,128)} %broadcast_in_dim.4), calls=%async_computation.4 | async-start | bytes 65536 | tf_op jit(solution)/shard_map/all_to_all | solution.py:115
  128.0 14.6 %all-to-all-start.4 = ((f32[24,1,256]{2,1,0:T(1,128)}), f32[24,1,256]{2,1,0:T(1,128)S(1)}, u32[]{:S(2)}, u32[]{:S(2)}) async-start(f32[24,1,256]{2,1,0:T(1,128)} %broadcast_in_dim.10), calls=%async_computation.5 | async-start | bytes 49152 | tf_op jit(solution)/shard_map/all_to_all | solution.py:115
  142.6 43.0 %all-to-all-start.1 = ((bf16[16,192,256]{2,1,0:T(8,128)(2,1)}), bf16[16,192,256]{2,1,0:T(8,128)(2,1)S(1)}, u32[]{:S(2)}, u32[]{:S(2)}) async-start(bf16[16,192,256]{2,1,0:T(8,128)(2,1)} %fusion.1), calls=%async_computation.2 | async-start | bytes 3145728 | tf_op jit(solution)/shard_map/all_to_all | solution.py:115
Sparse Core Ops, SparseCore 0:
  14.1 116.5 reduce-scatter.1

commit v2 on v1

v2 whole, which is shorter than its diff:
```python
import jax
import jax.numpy as jnp
from jax import lax
from jax.experimental import pallas as pl
from jax.experimental.pallas import tpu as pltpu
from jax.sharding import Mesh, PartitionSpec as P

XH, Y, CORE, XL, Z = 2, 8, 2, 2, 12
AXES = ("xh", "y", "c", "xl", "z")
DP, TENSOR = ("xh", "y", "c"), ("xl", "z")
TOK, D, COLS = 6, 6144, 256
Q, FQ = 4, 1536
GROUP = TOK * XL * Z
ROWS = GROUP * Q
HALF = ROWS // 2
CHUNK = TOK * Q
BLOCK = 384
OWNED = BLOCK // 2
NT = (((1,), (1,)), ((), ()))
TN = (((0,), (0,)), ((), ()))
VMEM = pl.BlockSpec(memory_space=pltpu.VMEM)
SMEM = pl.BlockSpec(memory_space=pltpu.SMEM)
PARAMS = pltpu.CompilerParams(vmem_limit_bytes=40 * 2**20)


def grad_kernel(side_ref, cot_ref, w_ref, comm_ref, keep_ref, send_ref, wide):
    mine = pl.multiple_of(side_ref[0] * HALF, HALF)
    theirs = pl.multiple_of((1 - side_ref[0]) * HALF, HALF)
    for q in range(Q):
        part = lax.dot_general(cot_ref[...], w_ref[q], NT, preferred_element_type=jnp.float32)
        for b in range(BLOCK // 128):
            wide[b, pl.ds(q, GROUP, stride=Q), :] = part[:, b * 128 : (b + 1) * 128]
    for b in range(BLOCK // 128):
        lanes = slice(b * 128, (b + 1) * 128)
        keep_ref[:, lanes] = wide[b, pl.ds(mine, HALF), :].astype(jnp.bfloat16)
        send_ref[:, lanes] = wide[b, pl.ds(theirs, HALF), :].astype(jnp.bfloat16)
        starts = [x * HALF + z * CHUNK for z in range(Z) for x in range(XL)]
        ordered = jnp.concatenate([wide[b, start : start + CHUNK, :] for start in starts])
        comm_ref[:, lanes] = ordered.astype(jnp.bfloat16)


def grad_terms(side, cotangent, weight):
    half = jax.ShapeDtypeStruct((HALF, FQ), jnp.bfloat16)
    return pl.pallas_call(
        grad_kernel,
        grid=(FQ // BLOCK,),
        out_shape=(jax.ShapeDtypeStruct((ROWS, FQ), jnp.bfloat16), half, half),
        in_specs=[
            SMEM,
            pl.BlockSpec((GROUP, COLS), lambda i: (0, 0)),
            pl.BlockSpec((Q, BLOCK, COLS), lambda i: (0, i, 0)),
        ],
        out_specs=(
            pl.BlockSpec((ROWS, BLOCK), lambda i: (0, i)),
            pl.BlockSpec((HALF, BLOCK), lambda i: (0, i)),
            pl.BlockSpec((HALF, BLOCK), lambda i: (0, i)),
        ),
        scratch_shapes=[pltpu.VMEM((BLOCK // 128, ROWS, 128), jnp.float32)],
        compiler_params=PARAMS,
        cost_estimate=pl.CostEstimate(
            flops=2 * GROUP * D * COLS, bytes_accessed=5 * 2**20, transcendentals=0
        ),
    )(side, cotangent, weight.reshape(Q, FQ, COLS))


def row_inverse(squares, rows, tokens):
    rows[...] = squares
    total = jnp.zeros((tokens, 128), jnp.float32)
    for q in range(Q):
        total += rows[pl.ds(q, tokens, stride=Q), :]
    return lax.rsqrt(jnp.sum(total, axis=1, keepdims=True) / D + 1e-05)


def gain_kernel(own_ref, keep_ref, got_ref, part_ref, rows):
    squares = jnp.zeros((HALF, 128), jnp.float32)
    for b in range(FQ // 128):
        values = own_ref[:, b * 128 : (b + 1) * 128].astype(jnp.float32)
        squares += values * values
    inverse = row_inverse(squares, rows, GROUP // 2)
    for q in range(Q):
        rows[pl.ds(q, GROUP // 2, stride=Q), :] = jnp.broadcast_to(inverse, (GROUP // 2, 128))
    for b in range(FQ // 128):
        lanes = slice(b * 128, (b + 1) * 128)
        term = keep_ref[:, lanes].astype(jnp.float32) + got_ref[:, lanes].astype(jnp.float32)
        product = own_ref[:, lanes].astype(jnp.float32) * rows[...] * term
        total = jnp.sum(product.reshape(HALF // 8, 8, 128), axis=0)
        part_ref[:, lanes] = total[:Q] + total[Q:]


def gain_terms(own, keep, got):
    return pl.pallas_call(
        gain_kernel,
        out_shape=jax.ShapeDtypeStruct((Q, FQ), jnp.float32),
        in_specs=[VMEM] * 3,
        out_specs=VMEM,
        scratch_shapes=[pltpu.VMEM((HALF, 128), jnp.float32)],
        compiler_params=PARAMS,
        cost_estimate=pl.CostEstimate(flops=5 * 2**20, bytes_accessed=4 * 2**20, transcendentals=0),
    )(own, keep, got)


def main_kernel(
    side_ref, own_ref, other_ref, w_ref, cot_ref, gain_ref,
    proj_ref, keep_ref, send_ref, wide, rows,
):
    mine = pl.multiple_of(side_ref[0] * HALF, HALF)
    theirs = pl.multiple_of((1 - side_ref[0]) * HALF, HALF)
    for b in range(FQ // 128):
        wide[b, pl.ds(mine, HALF), :] = own_ref[:, b * 128 : (b + 1) * 128].astype(jnp.float32)
        wide[b, pl.ds(theirs, HALF), :] = other_ref[:, b * 128 : (b + 1) * 128].astype(jnp.float32)
    squares = jnp.zeros((ROWS, 128), jnp.float32)
    for b in range(FQ // 128):
        squares += wide[b] * wide[b]
    inverse = row_inverse(squares, rows, GROUP)
    total = jnp.zeros((GROUP, COLS), jnp.float32)
    for p in range(D // BLOCK):
        q, first = divmod(p * BLOCK, FQ)
        pieces = []
        for b in range(BLOCK // 128):
            at = p * BLOCK + b * 128
            unit = wide[first // 128 + b, pl.ds(q, GROUP, stride=Q), :] * inverse
            normed = unit * gain_ref[:, at : at + 128]
            scale = (jnp.max(jnp.abs(normed), axis=1, keepdims=True) + 1e-06) / 448.0
            payload = (normed / scale).astype(jnp.bfloat16)
            pieces.append((payload.astype(jnp.float32) * scale).astype(jnp.bfloat16))
        restored = jnp.concatenate(pieces, axis=1)
        total += jnp.dot(
            restored, w_ref[p * BLOCK : (p + 1) * BLOCK, :], preferred_element_type=jnp.float32
        )
        product = lax.dot_general(
            restored, cot_ref[...], TN, preferred_element_type=jnp.float32
        ).astype(jnp.bfloat16)
        low, high = product[:OWNED], product[OWNED:]
        keep_ref[p] = jnp.where(side_ref[1] == 0, low, high)
        send_ref[p] = jnp.where(side_ref[1] == 0, high, low)
    proj_ref[...] = total.astype(jnp.bfloat16)


def main_products(side, own, other, weight, cotangent, gain):
    share = jax.ShapeDtypeStruct((XH * Y, OWNED, COLS), jnp.bfloat16)
    return pl.pallas_call(
        main_kernel,
        out_shape=(jax.ShapeDtypeStruct((GROUP, COLS), jnp.bfloat16), share, share),
        in_specs=[SMEM] + [VMEM] * 5,
        out_specs=(VMEM,) * 3,
        scratch_shapes=[
            pltpu.VMEM((FQ // 128, ROWS, 128), jnp.float32),
            pltpu.VMEM((ROWS, 128), jnp.float32),
        ],
        compiler_params=PARAMS,
        cost_estimate=pl.CostEstimate(
            flops=4 * GROUP * D * COLS, bytes_accessed=12 * 2**20, transcendentals=0
        ),
    )(side, own, other, weight, cotangent, gain)


def exchange(array, axes):
    return lax.all_to_all(array, axes, 0, 0, tiled=True)


def swap(array, axis):
    return lax.ppermute(array, axis, [(0, 1), (1, 0)])


def body(tokens, norm_gain, proj_weight, cotangent):
    side = jnp.stack([lax.axis_index("xl"), lax.axis_index("c")]).astype(jnp.int32)

    comm, grad_keep, grad_send = grad_terms(side, cotangent, proj_weight)
    grad_rows = lax.psum_scatter(comm, "z", scatter_dimension=0, tiled=True)
    grad_got = swap(grad_send, "xl")
    chunk, grad_keep = lax.optimization_barrier((tokens.reshape(TOK * Q, FQ), grad_keep))
    own = lax.all_gather(chunk, "z", axis=0, tiled=True)
    other = swap(own, "xl")

    part = gain_terms(own, grad_keep, grad_got)
    part = jnp.broadcast_to(part.reshape(D // 128, 128), (Y, D // 128, 128))
    part = jnp.sum(exchange(part, "y"), axis=0)
    other, part, grad_rows = lax.optimization_barrier((other, part, grad_rows))
    part = part + swap(part, "c")
    projected, keep, send = main_products(
        side, own, other, proj_weight, cotangent, norm_gain.reshape(1, D)
    )
    share = keep + swap(send, "c")
    share, part = lax.optimization_barrier((share, part))
    weight_grad = jnp.sum(exchange(share, ("xh", "y")).astype(jnp.float32), axis=0)
    part = jnp.sum(lax.all_gather(part, "z"), axis=0)
    part = part + swap(part, "xl")
    gain_grad = (part + swap(part, "xh")).reshape(D)

    values = tokens.astype(jnp.float32)
    rsq = lax.rsqrt(jnp.mean(values * values, axis=-1, keepdims=True) + 1e-05)
    unit_rows = values * rsq
    grad_rows = grad_rows.reshape(XL, TOK, D)
    is_low = side[0] == 0
    grad_rows, moved = (
        jnp.where(is_low, grad_rows[0], grad_rows[1]),
        jnp.where(is_low, grad_rows[1], grad_rows[0]),
    )
    normed_grad = grad_rows.astype(jnp.float32) + swap(moved, "xl").astype(jnp.float32)
    scaled = normed_grad * norm_gain
    input_grad = (
        rsq * (scaled - unit_rows * jnp.mean(scaled * unit_rows, axis=-1, keepdims=True))
    ).astype(jnp.bfloat16)
    return projected, input_grad, weight_grad, gain_grad


def solution(mesh):
    fine = Mesh(mesh.devices.reshape(XH, Y, CORE, XL, Z), AXES)
    return jax.shard_map(
        body,
        mesh=fine,
        in_specs=(P(DP + TENSOR, None), P(), P(None, TENSOR), P(DP, TENSOR)),
        out_specs=(P(DP, TENSOR), P(DP + TENSOR, None), P(DP, TENSOR), P()),
        check_vma=False,
    )
```

time: 195 us -> 162 us (0.83)
  the two profiles are of different devices: /device:TPU:8 before, /device:TPU:20 now
where the time goes in v2:
time: 162 us; the launch traced here: 161 us
  blocking collectives  79.4 us (49%)
  starting transfers between devices  27.9 us (17%)
  waiting for transfers between devices  18.4 us (11%)
  between operations  14.2 us (9%)
  Pallas kernels  11.3 us (7%)
  local copies, waits for them, and re-layouts  5.1 us (3%)
  other arithmetic  5.07 us (3%)
    all_gather x1, blocking collectives, body(): own = lax.all_gather(chunk, 'z', axis=0, tiled=True)  42.6 us
    all_gather x1, blocking collectives, body(): part = jnp.sum(lax.all_gather(part, 'z'), axis=0)  22.4 us
    ppermute x7, starting transfers between devices, swap(): return lax.ppermute(array, axis, [(0, 1), (1, 0)])  17.8 us
    ppermute x7, waiting for transfers between devices, swap(): return lax.ppermute(array, axis, [(0, 1), (1, 0)])  17.1 us
    all_to_all x1, blocking collectives, exchange(): return lax.all_to_all(array, axes, 0, 0, tiled=True)  14.4 us
    all_to_all x1, starting transfers between devices, exchange(): return lax.all_to_all(array, axes, 0, 0, tiled=True)  10 us
    pallas_call x1, Pallas kernels, main_products(): pl.pallas_call(main_kernel, out_shape=(jax.ShapeDtypeStruct((GROUP, COLS)...  5.27 us
    unnamed x20, local copies, waits for them, and re-layouts  4.89 us
  transfers between devices with their start and end apart: 9, of which 5 were waited for; matrix products, arithmetic and copies ran while one was open for 2% of the time, Pallas kernels for 1%

profile of v2, /device:TPU:20, one launch (start us, length us, event | category | flops | bytes accessed | tf_op | source)
XLA Modules:
  0.0 161.4 jit_solution(13135423085994965904)
XLA Ops:
  7.2 0.1 pad_add_fusion.side_ref
  7.3 1.9 %copy-done = bf16[6144,256]{1,0:T(8,128)(2,1)S(1)} copy-done((bf16[6144,256]{1,0:T(8,128)(2,1)S(1)}, bf16[6144,256]{1,0:T(8,128)(2,1)}, u32[]{:S(2)}) %copy-start) | copy-done | bytes 3145752
  9.2 0.9 copy-done.4
  10.1 3.9 %shard_map.75 = (bf16[576,1536]{1,0:T(8,128)(2,1)}, bf16[288,1536]{1,0:T(8,128)(2,1)S(1)}, bf16[288,1536]{1,0:T(8,128)(2,1)}) custom-call(s32[2]{0:T(128)S(1)} %pad_add_fusion.side_ref, bf16[144,256]{1,0:T(8,128)(2,1)S(1)} %copy-done.4, bf16[4,1536,256]{2,1,0:T(8,128)(2,1)S(1)} %bitcast.7), custom_call_target="tpu_custom_call" | custom-call | flops 452984832 | bytes 5242880 | tf_op jit(solution)/shard_map/pallas_call | solution.py:44
  14.0 0.9 copy-done.2
  14.9 3.2 %collective-permute-start.1 = (bf16[288,1536]{1,0:T(8,128)(2,1)}, bf16[288,1536]{1,0:T(8,128)(2,1)}, u32[]{:S(2)}, u32[]{:S(2)}) collective-permute-start(bf16[288,1536]{1,0:T(8,128)(2,1)} %get-tuple-element.20), channel_id=1, source_target_pairs={{0,12},{12,0},{1,13},{13,1},{2,14},{14,2},{3,15},{15,3},{4,16},{16... | collective-permute-start | bytes 2654216 | tf_op jit(solution)/shard_map/ppermute | solution.py:162
  18.3 42.6 %all_gather.9.own_ref = bf16[288,1536]{1,0:T(8,128)(2,1)} all-gather(bf16[24,1536]{1,0:T(8,128)(2,1)S(1)} %reshape.47), channel_id=1, replica_groups=mesh['xh'=2,'y'=8,'c'=2,'xl'=2,'z'=12] {'z'}, dimensions={0}, use_global_device_ids=true | all-gather | bytes 958464 | tf_op jit(solution)/shard_map/all_gather | solution.py:172
  60.9 2.3 %collective-permute-start = (bf16[288,1536]{1,0:T(8,128)(2,1)}, bf16[288,1536]{1,0:T(8,128)(2,1)}, u32[]{:S(2)}, u32[]{:S(2)}) collective-permute-start(bf16[288,1536]{1,0:T(8,128)(2,1)} %all_gather.9.own_ref), channel_id=1, source_target_pairs={{0,12},{12,0},{1,13},{13,1},{2,14},{14,2},{3,15},{15,3},{4,16},{16... | collective-permute-start | bytes 2654216 | tf_op jit(solution)/shard_map/ppermute | solution.py:162
  63.2 1.2 copy-done.3
  64.4 2.1 %shard_map.76 = f32[4,1536]{1,0:T(4,128)S(1)} custom-call(bf16[288,1536]{1,0:T(8,128)(2,1)} %all_gather.9.own_ref, bf16[288,1536]{1,0:T(8,128)(2,1)S(1)} %copy-done.3, bf16[288,1536]{1,0:T(8,128)(2,1)} %collective-permute-done.1.got_ref), custom_call_target="tpu_custom_call" | custom-call | flops 5242880 | bytes 4194304 | tf_op jit(solution)/shard_map/pallas_call | solution.py:91
  66.5 14.4 %all_to_all.10 = f32[8,48,128]{2,1,0:T(8,128)S(1)} all-to-all(f32[8,48,128]{2,1,0:T(8,128)S(1)} %broadcast_in_dim.2), channel_id=1, replica_groups=mesh['xh'=2,'y'=8,'c'=2,'xl'=2,'z'=12] {'y'}, dimensions={0} | all-to-all | bytes 393216 | tf_op jit(solution)/shard_map/all_to_all | solution.py:158
  80.9 0.6 reduce_sum.45
  81.5 1.3 reduce-scatter.2.cloned.1.call-done
  82.9 5.3 %shard_map.77 = (bf16[144,256]{1,0:T(8,128)(2,1)}, bf16[16,192,256]{2,1,0:T(8,128)(2,1)S(1)}, bf16[16,192,256]{2,1,0:T(8,128)(2,1)S(1)}) custom-call(s32[2]{0:T(128)S(1)} %pad_add_fusion.side_ref, bf16[288,1536]{1,0:T(8,128)(2,1)} %all_gather.9.own_ref, bf16[288,1536]{1,0:T(8,128)(2,1)} %collective-permute-done.other_ref, bf16[6144,256]{1,0:T(8,128)(2,1)S(1)} %copy-done.1, ...), custom_call_target="tpu_custom_call" | custom-call | flops 905969664 | bytes 12582912 | tf_op jit(solution)/shard_map/pallas_call | solution.py:141
  88.1 1.9 %collective-permute-start.3 = (bf16[16,192,256]{2,1,0:T(8,128)(2,1)S(1)}, bf16[16,192,256]{2,1,0:T(8,128)(2,1)S(1)}, u32[]{:S(2)}, u32[]{:S(2)}) collective-permute-start(bf16[16,192,256]{2,1,0:T(8,128)(2,1)S(1)} %get-tuple-element.26), channel_id=1, source_target_pairs={{0,24},{24,0},{1,25},{25,1},{2,26},{26,2},{3,27},{27,3},{4,28},{28... | collective-permute-start | bytes 4718600 | tf_op jit(solution)/shard_map/ppermute | solution.py:162
  90.1 2.4 %collective-permute-start.4 = (f32[48,128]{1,0:T(8,128)S(1)}, f32[48,128]{1,0:T(8,128)S(1)}, u32[]{:S(2)}, u32[]{:S(2)}) collective-permute-start(f32[48,128]{1,0:T(8,128)S(1)} %copy-done.9), channel_id=1, source_target_pairs={{0,24},{24,0},{1,25},{25,1},{2,26},{26,2},{3,27},{27,3},{4,28},{28... | collective-permute-start | bytes 73736 | tf_op jit(solution)/shard_map/ppermute | solution.py:162
  92.5 1.0 collective-permute-done.4
  93.5 1.7 %add.27 = bf16[16,192,256]{2,1,0:T(8,128)(2,1)} add(bf16[16,192,256]{2,1,0:T(8,128)(2,1)S(1)} %get-tuple-element.25, bf16[16,192,256]{2,1,0:T(8,128)(2,1)S(1)} %collective-permute-done.3) | non-fusion elementwise | flops 786432 | bytes 4718592 | tf_op jit(solution)/shard_map/add | solution.py:183
  95.1 10.0 %all-to-all-start.1 = ((bf16[16,192,256]{2,1,0:T(8,128)(2,1)}), bf16[16,192,256]{2,1,0:T(8,128)(2,1)S(1)}, u32[]{:S(2)}, u32[]{:S(2)}) async-start(bf16[16,192,256]{2,1,0:T(8,128)(2,1)} %add.27), calls=%async_computation.2 | async-start | bytes 3145728 | tf_op jit(solution)/shard_map/all_to_all | solution.py:158
  105.2 0.2 fusion.6
  105.4 3.0 %collective-permute-start.2 = (bf16[6,6144]{1,0:T(8,128)(2,1)S(1)}, bf16[6,6144]{1,0:T(8,128)(2,1)S(1)}, u32[]{:S(2)}, u32[]{:S(2)}) collective-permute-start(bf16[6,6144]{1,0:T(8,128)(2,1)S(1)} %select_n.19), channel_id=1, source_target_pairs={{0,12},{12,0},{1,13},{13,1},{2,14},{14,2},{3,15},{15,3},{4,16},{16... | collective-permute-start | bytes 221192 | tf_op jit(solution)/shard_map/ppermute | solution.py:162
  108.4 0.1 reshape.52
  108.5 9.0 %collective-permute-done.2 = bf16[6,6144]{1,0:T(8,128)(2,1)S(1)} collective-permute-done((bf16[6,6144]{1,0:T(8,128)(2,1)S(1)}, bf16[6,6144]{1,0:T(8,128)(2,1)S(1)}, u32[]{:S(2)}, u32[]{:S(2)}) %collective-permute-start.2) | collective-permute-done | bytes 73760 | tf_op jit(solution)/shard_map/ppermute | solution.py:162
  117.5 0.2 fusion.2
  117.7 22.4 %all-gather = f32[576,128]{1,0:T(8,128)S(1)} all-gather(f32[48,128]{1,0:T(8,128)S(1)} %add.28), channel_id=2, replica_groups=mesh['xh'=2,'y'=8,'c'=2,'xl'=2,'z'=12] {'z'}, dimensions={0}, use_global_device_ids=true | all-gather | bytes 319488 | tf_op jit(solution)/shard_map/all_gather | solution.py:186
  140.1 2.9 %collective-permute-start.5 = (f32[48,128]{1,0:T(8,128)S(1)}, f32[48,128]{1,0:T(8,128)S(1)}, u32[]{:S(2)}, u32[]{:S(2)}) collective-permute-start(f32[48,128]{1,0:T(8,128)S(1)} %reduce_sum.49), channel_id=1, source_target_pairs={{0,12},{12,0},{1,13},{13,1},{2,14},{14,2},{3,15},{15,3},{4,16},{16... | collective-permute-start | bytes 73736 | tf_op jit(solution)/shard_map/ppermute | solution.py:162
  143.0 2.8 %collective-permute-done.5 = f32[48,128]{1,0:T(8,128)S(1)} collective-permute-done((f32[48,128]{1,0:T(8,128)S(1)}, f32[48,128]{1,0:T(8,128)S(1)}, u32[]{:S(2)}, u32[]{:S(2)}) %collective-permute-start.5) | collective-permute-done | bytes 24608 | tf_op jit(solution)/shard_map/ppermute | solution.py:162
  145.8 2.2 %collective-permute-start.6 = (f32[48,128]{1,0:T(8,128)S(1)}, f32[48,128]{1,0:T(8,128)S(1)}, u32[]{:S(2)}, u32[]{:S(2)}) collective-permute-start(f32[48,128]{1,0:T(8,128)S(1)} %add.29), channel_id=1, source_target_pairs={{0,384},{384,0},{1,385},{385,1},{2,386},{386,2},{3,387},{387,3},{4... | collective-permute-start | bytes 73736 | tf_op jit(solution)/shard_map/ppermute | solution.py:162
  148.0 0.7 fusion.5
  148.8 4.3 %collective-permute-done.6 = f32[48,128]{1,0:T(8,128)S(1)} collective-permute-done((f32[48,128]{1,0:T(8,128)S(1)}, f32[48,128]{1,0:T(8,128)S(1)}, u32[]{:S(2)}, u32[]{:S(2)}) %collective-permute-start.6) | collective-permute-done | bytes 24608 | tf_op jit(solution)/shard_map/ppermute | solution.py:162
  153.0 0.6 add_bitcast_fusion
  153.7 0.9 convert_reduce_fusion
  (32 shorter events, 0.3 us)
Async XLA Ops:
  7.2 75.7 %reduce-scatter.2.cloned.1.call-start = ((), (), s32[]{:S(2)}) async-start(), calls=%async_computation.3 | async-start | bytes 1916928 | tf_op jit(solution)/shard_map/reduce_scatter | solution.py:169
  7.3 1.9 %copy-start = (bf16[6144,256]{1,0:T(8,128)(2,1)S(1)}, bf16[6144,256]{1,0:T(8,128)(2,1)}, u32[]{:S(2)}) copy-start(bf16[6144,256]{1,0:T(8,128)(2,1)} %w_ref.1) | copy-start | bytes 9437188
  9.2 0.9 copy-start.4
  14.0 0.9 copy-start.2
  14.9 3.3 %copy-start.7 = (bf16[6,6144]{1,0:T(8,128)(2,1)S(1)}, bf16[6,6144]{1,0:T(8,128)(2,1)}, u32[]{:S(2)}) copy-start(bf16[6,6144]{1,0:T(8,128)(2,1)} %param.4) | copy-start | bytes 221188
  14.9 48.3 %collective-permute-start.1 = (bf16[288,1536]{1,0:T(8,128)(2,1)}, bf16[288,1536]{1,0:T(8,128)(2,1)}, u32[]{:S(2)}, u32[]{:S(2)}) collective-permute-start(bf16[288,1536]{1,0:T(8,128)(2,1)} %get-tuple-element.20), channel_id=1, source_target_pairs={{0,12},{12,0},{1,13},{13,1},{2,14},{14,2},{3,15},{15,3},{4,16},{16... | collective-permute-start | bytes 2654216 | tf_op jit(solution)/shard_map/ppermute | solution.py:162
  18.3 64.6 %copy-start.5 = (bf16[144,256]{1,0:T(8,128)(2,1)S(1)}, bf16[144,256]{1,0:T(8,128)(2,1)}, u32[]{:S(2)}) copy-start(bf16[144,256]{1,0:T(8,128)(2,1)} %cot_ref.3) | copy-start | bytes 221188
  18.3 64.6 %copy-start.6 = (f32[6144]{0:T(1024)S(1)}, f32[6144]{0:T(1024)}, u32[]{:S(2)}) copy-start(f32[6144]{0:T(1024)} %param.5) | copy-start | bytes 73732
  60.9 21.9 %copy-start.1 = (bf16[6144,256]{1,0:T(8,128)(2,1)S(1)}, bf16[6144,256]{1,0:T(8,128)(2,1)}, u32[]{:S(2)}) copy-start(bf16[6144,256]{1,0:T(8,128)(2,1)} %w_ref.1) | copy-start | bytes 9437188
  60.9 20.6 %collective-permute-start = (bf16[288,1536]{1,0:T(8,128)(2,1)}, bf16[288,1536]{1,0:T(8,128)(2,1)}, u32[]{:S(2)}, u32[]{:S(2)}) collective-permute-start(bf16[288,1536]{1,0:T(8,128)(2,1)} %all_gather.9.own_ref), channel_id=1, source_target_pairs={{0,12},{12,0},{1,13},{13,1},{2,14},{14,2},{3,15},{15,3},{4,16},{16... | collective-permute-start | bytes 2654216 | tf_op jit(solution)/shard_map/ppermute | solution.py:162
  63.2 1.2 copy-start.3
  82.9 7.2 %copy-start.9 = (f32[48,128]{1,0:T(8,128)S(1)}, f32[48,128]{1,0:T(8,128)}, u32[]{:S(2)}) copy-start(f32[48,128]{1,0:T(8,128)} %reduce_sum.45) | copy-start | bytes 73732
  88.1 5.3 %collective-permute-start.3 = (bf16[16,192,256]{2,1,0:T(8,128)(2,1)S(1)}, bf16[16,192,256]{2,1,0:T(8,128)(2,1)S(1)}, u32[]{:S(2)}, u32[]{:S(2)}) collective-permute-start(bf16[16,192,256]{2,1,0:T(8,128)(2,1)S(1)} %get-tuple-element.26), channel_id=1, source_target_pairs={{0,24},{24,0},{1,25},{25,1},{2,26},{26,2},{3,27},{27,3},{4,28},{28... | collective-permute-start | bytes 4718600 | tf_op jit(solution)/shard_map/ppermute | solution.py:162
  90.1 3.4 %collective-permute-start.4 = (f32[48,128]{1,0:T(8,128)S(1)}, f32[48,128]{1,0:T(8,128)S(1)}, u32[]{:S(2)}, u32[]{:S(2)}) collective-permute-start(f32[48,128]{1,0:T(8,128)S(1)} %copy-done.9), channel_id=1, source_target_pairs={{0,24},{24,0},{1,25},{25,1},{2,26},{26,2},{3,27},{27,3},{4,28},{28... | collective-permute-start | bytes 73736 | tf_op jit(solution)/shard_map/ppermute | solution.py:162
  95.1 10.2 %copy-start.8 = (bf16[48,1536]{1,0:T(8,128)(2,1)S(1)}, bf16[48,1536]{1,0:T(8,128)(2,1)}, u32[]{:S(2)}) copy-start(bf16[48,1536]{1,0:T(8,128)(2,1)} %reduce-scatter.2.cloned.1.call-done) | copy-start | bytes 442372
  95.1 58.5 %all-to-all-start.1 = ((bf16[16,192,256]{2,1,0:T(8,128)(2,1)}), bf16[16,192,256]{2,1,0:T(8,128)(2,1)S(1)}, u32[]{:S(2)}, u32[]{:S(2)}) async-start(bf16[16,192,256]{2,1,0:T(8,128)(2,1)} %add.27), calls=%async_computation.2 | async-start | bytes 3145728 | tf_op jit(solution)/shard_map/all_to_all | solution.py:158
  105.4 12.0 %collective-permute-start.2 = (bf16[6,6144]{1,0:T(8,128)(2,1)S(1)}, bf16[6,6144]{1,0:T(8,128)(2,1)S(1)}, u32[]{:S(2)}, u32[]{:S(2)}) collective-permute-start(bf16[6,6144]{1,0:T(8,128)(2,1)S(1)} %select_n.19), channel_id=1, source_target_pairs={{0,12},{12,0},{1,13},{13,1},{2,14},{14,2},{3,15},{15,3},{4,16},{16... | collective-permute-start | bytes 221192 | tf_op jit(solution)/shard_map/ppermute | solution.py:162
  140.1 5.7 %collective-permute-start.5 = (f32[48,128]{1,0:T(8,128)S(1)}, f32[48,128]{1,0:T(8,128)S(1)}, u32[]{:S(2)}, u32[]{:S(2)}) collective-permute-start(f32[48,128]{1,0:T(8,128)S(1)} %reduce_sum.49), channel_id=1, source_target_pairs={{0,12},{12,0},{1,13},{13,1},{2,14},{14,2},{3,15},{15,3},{4,16},{16... | collective-permute-start | bytes 73736 | tf_op jit(solution)/shard_map/ppermute | solution.py:162
  145.8 7.2 %collective-permute-start.6 = (f32[48,128]{1,0:T(8,128)S(1)}, f32[48,128]{1,0:T(8,128)S(1)}, u32[]{:S(2)}, u32[]{:S(2)}) collective-permute-start(f32[48,128]{1,0:T(8,128)S(1)} %add.29), channel_id=1, source_target_pairs={{0,384},{384,0},{1,385},{385,1},{2,386},{386,2},{3,387},{387,3},{4... | collective-permute-start | bytes 73736 | tf_op jit(solution)/shard_map/ppermute | solution.py:162
Sparse Core Ops, SparseCore 0:
  15.1 67.7 reduce-scatter.1

commit v3 on v2

--- a/solution.py
+++ b/solution.py
@@ -19,13 +19,14 @@
 NT = (((1,), (1,)), ((), ()))
 TN = (((0,), (0,)), ((), ()))
 VMEM = pl.BlockSpec(memory_space=pltpu.VMEM)
-SMEM = pl.BlockSpec(memory_space=pltpu.SMEM)
 PARAMS = pltpu.CompilerParams(vmem_limit_bytes=40 * 2**20)
-
-
-def grad_kernel(side_ref, cot_ref, w_ref, comm_ref, keep_ref, send_ref, wide):
-    mine = pl.multiple_of(side_ref[0] * HALF, HALF)
-    theirs = pl.multiple_of((1 - side_ref[0]) * HALF, HALF)
+STREAMED = pltpu.CompilerParams(vmem_limit_bytes=60 * 2**20)
+
+
+def grad_kernel(cot_ref, w_ref, comm_ref, keep_ref, send_ref, wide):
+    side = lax.axis_index("xl")
+    mine = pl.multiple_of(side * HALF, HALF)
+    theirs = pl.multiple_of((1 - side) * HALF, HALF)
     for q in range(Q):
         part = lax.dot_general(cot_ref[...], w_ref[q], NT, preferred_element_type=jnp.float32)
         for b in range(BLOCK // 128):
@@ -39,14 +40,13 @@
         comm_ref[:, lanes] = ordered.astype(jnp.bfloat16)
 
 
-def grad_terms(side, cotangent, weight):
+def grad_terms(cotangent, weight):
     half = jax.ShapeDtypeStruct((HALF, FQ), jnp.bfloat16)
     return pl.pallas_call(
         grad_kernel,
         grid=(FQ // BLOCK,),
         out_shape=(jax.ShapeDtypeStruct((ROWS, FQ), jnp.bfloat16), half, half),
         in_specs=[
-            SMEM,
             pl.BlockSpec((GROUP, COLS), lambda i: (0, 0)),
             pl.BlockSpec((Q, BLOCK, COLS), lambda i: (0, i, 0)),
         ],
@@ -56,11 +56,11 @@
             pl.BlockSpec((HALF, BLOCK), lambda i: (0, i)),
         ),
         scratch_shapes=[pltpu.VMEM((BLOCK // 128, ROWS, 128), jnp.float32)],
-        compiler_params=PARAMS,
+        compiler_params=STREAMED,
         cost_estimate=pl.CostEstimate(
             flops=2 * GROUP * D * COLS, bytes_accessed=5 * 2**20, transcendentals=0
         ),
-    )(side, cotangent, weight.reshape(Q, FQ, COLS))
+    )(cotangent, weight.reshape(Q, FQ, COLS))
 
 
 def row_inverse(squares, rows, tokens):
@@ -100,19 +100,20 @@
 
 
 def main_kernel(
-    side_ref, own_ref, other_ref, w_ref, cot_ref, gain_ref,
-    proj_ref, keep_ref, send_ref, wide, rows,
+    own_ref, other_ref, cot_ref, gain_ref,
+    restored_ref, keep_ref, send_ref, wide, rows,
 ):
-    mine = pl.multiple_of(side_ref[0] * HALF, HALF)
-    theirs = pl.multiple_of((1 - side_ref[0]) * HALF, HALF)
+    side = lax.axis_index("xl")
+    mine = pl.multiple_of(side * HALF, HALF)
+    theirs = pl.multiple_of((1 - side) * HALF, HALF)
     for b in range(FQ // 128):
         wide[b, pl.ds(mine, HALF), :] = own_ref[:, b * 128 : (b + 1) * 128].astype(jnp.float32)
         wide[b, pl.ds(theirs, HALF), :] = other_ref[:, b * 128 : (b + 1) * 128].astype(jnp.float32)
+    core = lax.axis_index("c")
     squares = jnp.zeros((ROWS, 128), jnp.float32)
     for b in range(FQ // 128):
         squares += wide[b] * wide[b]
     inverse = row_inverse(squares, rows, GROUP)
-    total = jnp.zeros((GROUP, COLS), jnp.float32)
     for p in range(D // BLOCK):
         q, first = divmod(p * BLOCK, FQ)
         pieces = []
@@ -124,24 +125,21 @@
             payload = (normed / scale).astype(jnp.bfloat16)
             pieces.append((payload.astype(jnp.float32) * scale).astype(jnp.bfloat16))
         restored = jnp.concatenate(pieces, axis=1)
-        total += jnp.dot(
-            restored, w_ref[p * BLOCK : (p + 1) * BLOCK, :], preferred_element_type=jnp.float32
-        )
+        restored_ref[:, p * BLOCK : (p + 1) * BLOCK] = restored
         product = lax.dot_general(
             restored, cot_ref[...], TN, preferred_element_type=jnp.float32
         ).astype(jnp.bfloat16)
         low, high = product[:OWNED], product[OWNED:]
-        keep_ref[p] = jnp.where(side_ref[1] == 0, low, high)
-        send_ref[p] = jnp.where(side_ref[1] == 0, high, low)
-    proj_ref[...] = total.astype(jnp.bfloat16)
-
-
-def main_products(side, own, other, weight, cotangent, gain):
+        keep_ref[p] = jnp.where(core == 0, low, high)
+        send_ref[p] = jnp.where(core == 0, high, low)
+
+
+def main_products(own, other, cotangent, gain):
     share = jax.ShapeDtypeStruct((XH * Y, OWNED, COLS), jnp.bfloat16)
     return pl.pallas_call(
         main_kernel,
-        out_shape=(jax.ShapeDtypeStruct((GROUP, COLS), jnp.bfloat16), share, share),
-        in_specs=[SMEM] + [VMEM] * 5,
+        out_shape=(jax.ShapeDtypeStruct((GROUP, D), jnp.bfloat16), share, share),
+        in_specs=[VMEM] * 4,
         out_specs=(VMEM,) * 3,
         scratch_shapes=[
             pltpu.VMEM((FQ // 128, ROWS, 128), jnp.float32),
@@ -149,9 +147,9 @@
         ],
         compiler_params=PARAMS,
         cost_estimate=pl.CostEstimate(
-            flops=4 * GROUP * D * COLS, bytes_accessed=12 * 2**20, transcendentals=0
+            flops=2 * GROUP * D * COLS, bytes_accessed=10 * 2**20, transcendentals=0
         ),
-    )(side, own, other, weight, cotangent, gain)
+    )(own, other, cotangent, gain)
 
 
 def exchange(array, axes):
@@ -163,9 +161,7 @@
 
 
 def body(tokens, norm_gain, proj_weight, cotangent):
-    side = jnp.stack([lax.axis_index("xl"), lax.axis_index("c")]).astype(jnp.int32)
-
-    comm, grad_keep, grad_send = grad_terms(side, cotangent, proj_weight)
+    comm, grad_keep, grad_send = grad_terms(cotangent, proj_weight)
     grad_rows = lax.psum_scatter(comm, "z", scatter_dimension=0, tiled=True)
     grad_got = swap(grad_send, "xl")
     chunk, grad_keep = lax.optimization_barrier((tokens.reshape(TOK * Q, FQ), grad_keep))
@@ -175,15 +171,18 @@
     part = gain_terms(own, grad_keep, grad_got)
     part = jnp.broadcast_to(part.reshape(D // 128, 128), (Y, D // 128, 128))
     part = jnp.sum(exchange(part, "y"), axis=0)
-    other, part, grad_rows = lax.optimization_barrier((other, part, grad_rows))
+    other, part = lax.optimization_barrier((other, part))
     part = part + swap(part, "c")
-    projected, keep, send = main_products(
-        side, own, other, proj_weight, cotangent, norm_gain.reshape(1, D)
+    restored, keep, send = main_products(own, other, cotangent, norm_gain.reshape(1, D))
+    share = keep + swap(send, "c")
+    projected = jnp.dot(restored, proj_weight, preferred_element_type=jnp.float32)
+    projected = projected.astype(jnp.bfloat16)
+    share, part, projected, grad_rows = lax.optimization_barrier(
+        (share, part, projected, grad_rows)
     )
-    share = keep + swap(send, "c")
-    share, part = lax.optimization_barrier((share, part))
     weight_grad = jnp.sum(exchange(share, ("xh", "y")).astype(jnp.float32), axis=0)
     part = jnp.sum(lax.all_gather(part, "z"), axis=0)
+    part, grad_rows = lax.optimization_barrier((part, grad_rows))
     part = part + swap(part, "xl")
     gain_grad = (part + swap(part, "xh")).reshape(D)
 
@@ -191,7 +190,7 @@
     rsq = lax.rsqrt(jnp.mean(values * values, axis=-1, keepdims=True) + 1e-05)
     unit_rows = values * rsq
     grad_rows = grad_rows.reshape(XL, TOK, D)
-    is_low = side[0] == 0
+    is_low = lax.axis_index("xl") == 0
     grad_rows, moved = (
         jnp.where(is_low, grad_rows[0], grad_rows[1]),
         jnp.where(is_low, grad_rows[1], grad_rows[0]),

time: 162 us -> 151 us (0.932)
  the two profiles are of different devices: /device:TPU:20 before, /device:TPU:40 now
where the time goes in v3:
time: 151 us; the launch traced here: 150 us
  blocking collectives  71.3 us (47%)
  starting transfers between devices  30.9 us (20%)
  waiting for transfers between devices  14.5 us (10%)
  between operations  14.2 us (9%)
  Pallas kernels  8.77 us (6%)
  other arithmetic  4.39 us (3%)
  local copies, waits for them, and re-layouts  3.19 us (2%)
  matrix products  3.15 us (2%)
    all_gather x1, blocking collectives, body(): own = lax.all_gather(chunk, 'z', axis=0, tiled=True)  39 us
    all_gather x1, blocking collectives, body(): part = jnp.sum(lax.all_gather(part, 'z'), axis=0)  21.2 us
    ppermute x7, starting transfers between devices, swap(): return lax.ppermute(array, axis, [(0, 1), (1, 0)])  21.1 us
    ppermute x7, waiting for transfers between devices, swap(): return lax.ppermute(array, axis, [(0, 1), (1, 0)])  14.4 us
    all_to_all x1, blocking collectives, exchange(): return lax.all_to_all(array, axes, 0, 0, tiled=True)  11.1 us
    all_to_all x1, starting transfers between devices, exchange(): return lax.all_to_all(array, axes, 0, 0, tiled=True)  9.77 us
    pallas_call x1, Pallas kernels, grad_terms(): pl.pallas_call(grad_kernel, grid=(FQ // BLOCK,), out_shape=(jax.ShapeDtyp...  5.31 us
    dot_general x1, matrix products, body(): jnp.dot(restored, proj_weight, preferred_element_type=jnp.float32)  3.15 us
  transfers between devices with their start and end apart: 9, of which 3 were waited for; matrix products, arithmetic and copies ran while one was open for 5% of the time, Pallas kernels for 2%

profile of v3, /device:TPU:40, one launch (start us, length us, event | category | flops | bytes accessed | tf_op | source)
XLA Modules:
  0.0 150.4 jit_solution(7259043290820376084)
XLA Ops:
  7.2 0.0 reduce-scatter.2.cloned.1.call-start
  7.2 5.3 %shard_map.75 = (bf16[576,1536]{1,0:T(8,128)(2,1)}, bf16[288,1536]{1,0:T(8,128)(2,1)}, bf16[288,1536]{1,0:T(8,128)(2,1)}) custom-call(bf16[144,256]{1,0:T(8,128)(2,1)} %cot_ref.3, bf16[4,1536,256]{2,1,0:T(8,128)(2,1)} %bitcast.8), custom_call_target="tpu_custom_call" | custom-call | flops 452984832 | bytes 5242880 | tf_op jit(solution)/shard_map/pallas_call | solution.py:45
  12.6 3.5 %collective-permute-start.1 = (bf16[288,1536]{1,0:T(8,128)(2,1)}, bf16[288,1536]{1,0:T(8,128)(2,1)S(1)}, u32[]{:S(2)}, u32[]{:S(2)}) collective-permute-start(bf16[288,1536]{1,0:T(8,128)(2,1)} %get-tuple-element.23), channel_id=1, source_target_pairs={{0,12},{12,0},{1,13},{13,1},{2,14},{14,2},{3,15},{15,3},{4,16},{16... | collective-permute-start | bytes 2654216 | tf_op jit(solution)/shard_map/ppermute | solution.py:160
  16.1 0.1 reshape.47
  16.2 39.0 %all_gather.9.own_ref = bf16[288,1536]{1,0:T(8,128)(2,1)S(1)} all-gather(bf16[24,1536]{1,0:T(8,128)(2,1)S(1)} %reshape.47), channel_id=1, replica_groups=mesh['xh'=2,'y'=8,'c'=2,'xl'=2,'z'=12] {'z'}, dimensions={0}, use_global_device_ids=true | all-gather | bytes 958464 | tf_op jit(solution)/shard_map/all_gather | solution.py:168
  55.2 3.0 %collective-permute-start = (bf16[288,1536]{1,0:T(8,128)(2,1)S(1)}, bf16[288,1536]{1,0:T(8,128)(2,1)S(1)}, u32[]{:S(2)}, u32[]{:S(2)}) collective-permute-start(bf16[288,1536]{1,0:T(8,128)(2,1)S(1)} %all_gather.9.own_ref), channel_id=1, source_target_pairs={{0,12},{12,0},{1,13},{13,1},{2,14},{14,2},{3,15},{15,3},{4,16},{16... | collective-permute-start | bytes 2654216 | tf_op jit(solution)/shard_map/ppermute | solution.py:160
  58.2 0.6 shard_map.76
  58.8 0.6 copy-done.4
  59.4 0.8 reshape.49
  60.2 11.1 %all_to_all.10 = f32[8,48,128]{2,1,0:T(8,128)S(1)} all-to-all(f32[8,48,128]{2,1,0:T(8,128)S(1)} %broadcast_in_dim.2), channel_id=1, replica_groups=mesh['xh'=2,'y'=8,'c'=2,'xl'=2,'z'=12] {'y'}, dimensions={0} | all-to-all | bytes 393216 | tf_op jit(solution)/shard_map/all_to_all | solution.py:156
  71.3 3.2 %collective-permute-done.other_ref = bf16[288,1536]{1,0:T(8,128)(2,1)S(1)} collective-permute-done((bf16[288,1536]{1,0:T(8,128)(2,1)S(1)}, bf16[288,1536]{1,0:T(8,128)(2,1)S(1)}, u32[]{:S(2)}, u32[]{:S(2)}) %collective-permute-start) | collective-permute-done | bytes 884768 | tf_op jit(solution)/shard_map/ppermute | solution.py:160
  74.5 0.9 copy-done.1
  75.4 0.7 copy-done.2
  76.1 2.8 %shard_map.77 = (bf16[144,6144]{1,0:T(8,128)(2,1)S(1)}, bf16[16,192,256]{2,1,0:T(8,128)(2,1)S(1)}, bf16[16,192,256]{2,1,0:T(8,128)(2,1)S(1)}) custom-call(bf16[288,1536]{1,0:T(8,128)(2,1)S(1)} %all_gather.9.own_ref, bf16[288,1536]{1,0:T(8,128)(2,1)S(1)} %collective-permute-done.other_ref, bf16[144,256]{1,0:T(8,128)(2,1)S(1)} %copy-done.1, f32[1,6144]{1,0:T(1,128)S(1)} %bitcast.7), custom_call_target="tpu_custom_call" | custom-call | flops 452984832 | bytes 10485760 | tf_op jit(solution)/shard_map/pallas_call | solution.py:139
  79.0 1.9 %collective-permute-start.2 = (bf16[16,192,256]{2,1,0:T(8,128)(2,1)S(1)}, bf16[16,192,256]{2,1,0:T(8,128)(2,1)S(1)}, u32[]{:S(2)}, u32[]{:S(2)}) collective-permute-start(bf16[16,192,256]{2,1,0:T(8,128)(2,1)S(1)} %get-tuple-element.26), channel_id=1, source_target_pairs={{0,24},{24,0},{1,25},{25,1},{2,26},{26,2},{3,27},{27,3},{4,28},{28... | collective-permute-start | bytes 4718600 | tf_op jit(solution)/shard_map/ppermute | solution.py:160
  80.9 2.4 %collective-permute-start.3 = (f32[48,128]{1,0:T(8,128)S(1)}, f32[48,128]{1,0:T(8,128)S(1)}, u32[]{:S(2)}, u32[]{:S(2)}) collective-permute-start(f32[48,128]{1,0:T(8,128)S(1)} %reduce_sum.45), channel_id=1, source_target_pairs={{0,24},{24,0},{1,25},{25,1},{2,26},{26,2},{3,27},{27,3},{4,28},{28... | collective-permute-start | bytes 73736 | tf_op jit(solution)/shard_map/ppermute | solution.py:160
  83.3 3.2 %convolution_convert_fusion = bf16[144,256]{1,0:T(8,128)(2,1)} fusion(bf16[144,6144]{1,0:T(8,128)(2,1)S(1)} %get-tuple-element.28, bf16[6144,256]{1,0:T(8,128)(2,1)} %param.6), kind=kOutput, calls=%fused_computation.1 | convolution fusion | flops 453021696 | bytes 4988928 | tf_op jit(solution)/shard_map/dot_general | solution.py:178
  86.5 1.7 %add.25 = bf16[16,192,256]{2,1,0:T(8,128)(2,1)} add(bf16[16,192,256]{2,1,0:T(8,128)(2,1)S(1)} %get-tuple-element.25, bf16[16,192,256]{2,1,0:T(8,128)(2,1)S(1)} %collective-permute-done.2) | non-fusion elementwise | flops 786432 | bytes 4718592 | tf_op jit(solution)/shard_map/add | solution.py:177
  88.1 9.8 %all-to-all-start.1 = ((bf16[16,192,256]{2,1,0:T(8,128)(2,1)}), bf16[16,192,256]{2,1,0:T(8,128)(2,1)S(1)}, u32[]{:S(2)}, u32[]{:S(2)}) async-start(bf16[16,192,256]{2,1,0:T(8,128)(2,1)} %add.25), calls=%async_computation.2 | async-start | bytes 3145728 | tf_op jit(solution)/shard_map/all_to_all | solution.py:156
  97.9 0.2 fusion.6
  98.1 21.2 %all-gather = f32[576,128]{1,0:T(8,128)S(1)} all-gather(f32[48,128]{1,0:T(8,128)S(1)} %add.26), channel_id=2, replica_groups=mesh['xh'=2,'y'=8,'c'=2,'xl'=2,'z'=12] {'z'}, dimensions={0}, use_global_device_ids=true | all-gather | bytes 319488 | tf_op jit(solution)/shard_map/all_gather | solution.py:184
  119.3 3.0 %collective-permute-start.5 = (f32[48,128]{1,0:T(8,128)S(1)}, f32[48,128]{1,0:T(8,128)S(1)}, u32[]{:S(2)}, u32[]{:S(2)}) collective-permute-start(f32[48,128]{1,0:T(8,128)S(1)} %reduce_sum.47), channel_id=1, source_target_pairs={{0,12},{12,0},{1,13},{13,1},{2,14},{14,2},{3,15},{15,3},{4,16},{16... | collective-permute-start | bytes 73736 | tf_op jit(solution)/shard_map/ppermute | solution.py:160
  122.3 7.8 %collective-permute-done.5 = f32[48,128]{1,0:T(8,128)S(1)} collective-permute-done((f32[48,128]{1,0:T(8,128)S(1)}, f32[48,128]{1,0:T(8,128)S(1)}, u32[]{:S(2)}, u32[]{:S(2)}) %collective-permute-start.5) | collective-permute-done | bytes 24608 | tf_op jit(solution)/shard_map/ppermute | solution.py:160
  130.1 5.0 %collective-permute-start.6 = (f32[48,128]{1,0:T(8,128)S(1)}, f32[48,128]{1,0:T(8,128)S(1)}, u32[]{:S(2)}, u32[]{:S(2)}) collective-permute-start(f32[48,128]{1,0:T(8,128)S(1)} %add.29), channel_id=1, source_target_pairs={{0,384},{384,0},{1,385},{385,1},{2,386},{386,2},{3,387},{387,3},{4... | collective-permute-start | bytes 73736 | tf_op jit(solution)/shard_map/ppermute | solution.py:160
  135.1 0.1 select_n.19
  135.1 2.3 %collective-permute-start.4 = (bf16[6,6144]{1,0:T(8,128)(2,1)S(1)}, bf16[6,6144]{1,0:T(8,128)(2,1)S(1)}, u32[]{:S(2)}, u32[]{:S(2)}) collective-permute-start(bf16[6,6144]{1,0:T(8,128)(2,1)S(1)} %select_n.19), channel_id=1, source_target_pairs={{0,12},{12,0},{1,13},{13,1},{2,14},{14,2},{3,15},{15,3},{4,16},{16... | collective-permute-start | bytes 221192 | tf_op jit(solution)/shard_map/ppermute | solution.py:160
  137.5 0.1 reshape.52
  137.6 0.6 add_bitcast_fusion
  138.2 3.5 %collective-permute-done.4 = bf16[6,6144]{1,0:T(8,128)(2,1)S(1)} collective-permute-done((bf16[6,6144]{1,0:T(8,128)(2,1)S(1)}, bf16[6,6144]{1,0:T(8,128)(2,1)S(1)}, u32[]{:S(2)}, u32[]{:S(2)}) %collective-permute-start.4) | collective-permute-done | bytes 73760 | tf_op jit(solution)/shard_map/ppermute | solution.py:160
  141.6 0.2 fusion.2
  141.9 0.7 fusion.5
  142.6 0.9 convert_reduce_fusion
  (28 shorter events, 0.2 us)
Async XLA Ops:
  7.2 81.0 %reduce-scatter.2.cloned.1.call-start = ((), (), s32[]{:S(2)}) async-start(), calls=%async_computation.3 | async-start | bytes 1916928 | tf_op jit(solution)/shard_map/reduce_scatter | solution.py:165
  7.2 8.9 %copy-start.5 = (bf16[6,6144]{1,0:T(8,128)(2,1)S(1)}, bf16[6,6144]{1,0:T(8,128)(2,1)}, u32[]{:S(2)}) copy-start(bf16[6,6144]{1,0:T(8,128)(2,1)} %param.4) | copy-start | bytes 221188
  12.5 45.6 %copy-start = (bf16[288,1536]{1,0:T(8,128)(2,1)S(1)}, bf16[288,1536]{1,0:T(8,128)(2,1)}, u32[]{:S(2)}) copy-start(bf16[288,1536]{1,0:T(8,128)(2,1)} %get-tuple-element.22.keep_ref) | copy-start | bytes 2654212
  12.6 45.6 %collective-permute-start.1 = (bf16[288,1536]{1,0:T(8,128)(2,1)}, bf16[288,1536]{1,0:T(8,128)(2,1)S(1)}, u32[]{:S(2)}, u32[]{:S(2)}) collective-permute-start(bf16[288,1536]{1,0:T(8,128)(2,1)} %get-tuple-element.23), channel_id=1, source_target_pairs={{0,12},{12,0},{1,13},{13,1},{2,14},{14,2},{3,15},{15,3},{4,16},{16... | collective-permute-start | bytes 2654216 | tf_op jit(solution)/shard_map/ppermute | solution.py:160
  55.2 19.3 %collective-permute-start = (bf16[288,1536]{1,0:T(8,128)(2,1)S(1)}, bf16[288,1536]{1,0:T(8,128)(2,1)S(1)}, u32[]{:S(2)}, u32[]{:S(2)}) collective-permute-start(bf16[288,1536]{1,0:T(8,128)(2,1)S(1)} %all_gather.9.own_ref), channel_id=1, source_target_pairs={{0,12},{12,0},{1,13},{13,1},{2,14},{14,2},{3,15},{15,3},{4,16},{16... | collective-permute-start | bytes 2654216 | tf_op jit(solution)/shard_map/ppermute | solution.py:160
  58.8 0.6 copy-start.4
  74.5 0.9 copy-start.1
  75.4 0.7 copy-start.2
  79.0 7.5 %collective-permute-start.2 = (bf16[16,192,256]{2,1,0:T(8,128)(2,1)S(1)}, bf16[16,192,256]{2,1,0:T(8,128)(2,1)S(1)}, u32[]{:S(2)}, u32[]{:S(2)}) collective-permute-start(bf16[16,192,256]{2,1,0:T(8,128)(2,1)S(1)} %get-tuple-element.26), channel_id=1, source_target_pairs={{0,24},{24,0},{1,25},{25,1},{2,26},{26,2},{3,27},{27,3},{4,28},{28... | collective-permute-start | bytes 4718600 | tf_op jit(solution)/shard_map/ppermute | solution.py:160
  80.9 5.6 %collective-permute-start.3 = (f32[48,128]{1,0:T(8,128)S(1)}, f32[48,128]{1,0:T(8,128)S(1)}, u32[]{:S(2)}, u32[]{:S(2)}) collective-permute-start(f32[48,128]{1,0:T(8,128)S(1)} %reduce_sum.45), channel_id=1, source_target_pairs={{0,24},{24,0},{1,25},{25,1},{2,26},{26,2},{3,27},{27,3},{4,28},{28... | collective-permute-start | bytes 73736 | tf_op jit(solution)/shard_map/ppermute | solution.py:160
  88.1 9.8 %copy-start.6 = (bf16[6,6144]{1,0:T(8,128)(2,1)S(1)}, bf16[6,6144]{1,0:T(8,128)(2,1)}, u32[]{:S(2)}) copy-start(bf16[6,6144]{1,0:T(8,128)(2,1)} %param.4) | copy-start | bytes 221188
  88.1 53.5 %copy-start.3 = (f32[6144]{0:T(1024)S(1)}, f32[6144]{0:T(1024)}, u32[]{:S(2)}) copy-start(f32[6144]{0:T(1024)} %param.5) | copy-start | bytes 73732
  88.1 46.9 %copy-start.7 = (bf16[48,1536]{1,0:T(8,128)(2,1)S(1)}, bf16[48,1536]{1,0:T(8,128)(2,1)}, u32[]{:S(2)}) copy-start(bf16[48,1536]{1,0:T(8,128)(2,1)} %reduce-scatter.2.cloned.1.call-done) | copy-start | bytes 442372
  88.1 54.5 %all-to-all-start.1 = ((bf16[16,192,256]{2,1,0:T(8,128)(2,1)}), bf16[16,192,256]{2,1,0:T(8,128)(2,1)S(1)}, u32[]{:S(2)}, u32[]{:S(2)}) async-start(bf16[16,192,256]{2,1,0:T(8,128)(2,1)} %add.25), calls=%async_computation.2 | async-start | bytes 3145728 | tf_op jit(solution)/shard_map/all_to_all | solution.py:156
  119.3 10.8 %collective-permute-start.5 = (f32[48,128]{1,0:T(8,128)S(1)}, f32[48,128]{1,0:T(8,128)S(1)}, u32[]{:S(2)}, u32[]{:S(2)}) collective-permute-start(f32[48,128]{1,0:T(8,128)S(1)} %reduce_sum.47), channel_id=1, source_target_pairs={{0,12},{12,0},{1,13},{13,1},{2,14},{14,2},{3,15},{15,3},{4,16},{16... | collective-permute-start | bytes 73736 | tf_op jit(solution)/shard_map/ppermute | solution.py:160
  130.1 7.5 %collective-permute-start.6 = (f32[48,128]{1,0:T(8,128)S(1)}, f32[48,128]{1,0:T(8,128)S(1)}, u32[]{:S(2)}, u32[]{:S(2)}) collective-permute-start(f32[48,128]{1,0:T(8,128)S(1)} %add.29), channel_id=1, source_target_pairs={{0,384},{384,0},{1,385},{385,1},{2,386},{386,2},{3,387},{387,3},{4... | collective-permute-start | bytes 73736 | tf_op jit(solution)/shard_map/ppermute | solution.py:160
  135.1 6.5 %collective-permute-start.4 = (bf16[6,6144]{1,0:T(8,128)(2,1)S(1)}, bf16[6,6144]{1,0:T(8,128)(2,1)S(1)}, u32[]{:S(2)}, u32[]{:S(2)}) collective-permute-start(bf16[6,6144]{1,0:T(8,128)(2,1)S(1)} %select_n.19), channel_id=1, source_target_pairs={{0,12},{12,0},{1,13},{13,1},{2,14},{14,2},{3,15},{15,3},{4,16},{16... | collective-permute-start | bytes 221192 | tf_op jit(solution)/shard_map/ppermute | solution.py:160
Sparse Core Ops, SparseCore 0:
  12.7 67.6 reduce-scatter.1

commit v4 on v3

--- a/solution.py
+++ b/solution.py
@@ -84,13 +84,16 @@
         term = keep_ref[:, lanes].astype(jnp.float32) + got_ref[:, lanes].astype(jnp.float32)
         product = own_ref[:, lanes].astype(jnp.float32) * rows[...] * term
         total = jnp.sum(product.reshape(HALF // 8, 8, 128), axis=0)
-        part_ref[:, lanes] = total[:Q] + total[Q:]
+        total = total[:Q] + total[Q:]
+        for q in range(Q):
+            row = q * (FQ // 128) + b
+            part_ref[:, row : row + 1, :] = jnp.broadcast_to(total[q : q + 1], (Y, 1, 128))
 
 
 def gain_terms(own, keep, got):
     return pl.pallas_call(
         gain_kernel,
-        out_shape=jax.ShapeDtypeStruct((Q, FQ), jnp.float32),
+        out_shape=jax.ShapeDtypeStruct((Y, D // 128, 128), jnp.float32),
         in_specs=[VMEM] * 3,
         out_specs=VMEM,
         scratch_shapes=[pltpu.VMEM((HALF, 128), jnp.float32)],
@@ -169,7 +172,6 @@
     other = swap(own, "xl")
 
     part = gain_terms(own, grad_keep, grad_got)
-    part = jnp.broadcast_to(part.reshape(D // 128, 128), (Y, D // 128, 128))
     part = jnp.sum(exchange(part, "y"), axis=0)
     other, part = lax.optimization_barrier((other, part))
     part = part + swap(part, "c")

time: 151 us -> 151 us (level)
  no operation moved by 1% of the time
where the time goes in v4:
time: 151 us; the launch traced here: 150 us
  blocking collectives  71.3 us (47%)
  starting transfers between devices  30.9 us (20%)
  waiting for transfers between devices  15.8 us (10%)
  between operations  14.2 us (9%)
  Pallas kernels  8.76 us (6%)
  other arithmetic  4.4 us (3%)
  matrix products  3.15 us (2%)
  local copies, waits for them, and re-layouts  1.82 us (1%)
    all_gather x1, blocking collectives, body(): own = lax.all_gather(chunk, 'z', axis=0, tiled=True)  39 us
    all_gather x1, blocking collectives, body(): part = jnp.sum(lax.all_gather(part, 'z'), axis=0)  21.2 us
    ppermute x7, starting transfers between devices, swap(): return lax.ppermute(array, axis, [(0, 1), (1, 0)])  21.1 us
    ppermute x7, waiting for transfers between devices, swap(): return lax.ppermute(array, axis, [(0, 1), (1, 0)])  15.8 us
    all_to_all x1, blocking collectives, exchange(): return lax.all_to_all(array, axes, 0, 0, tiled=True)  11.1 us
    all_to_all x1, starting transfers between devices, exchange(): return lax.all_to_all(array, axes, 0, 0, tiled=True)  9.77 us
    pallas_call x1, Pallas kernels, grad_terms(): pl.pallas_call(grad_kernel, grid=(FQ // BLOCK,), out_shape=(jax.ShapeDtyp...  5.27 us
    dot_general x1, matrix products, body(): jnp.dot(restored, proj_weight, preferred_element_type=jnp.float32)  3.15 us
  transfers between devices with their start and end apart: 9, of which 3 were waited for; matrix products, arithmetic and copies ran while one was open for 5% of the time, Pallas kernels for 2%

profile of v4, /device:TPU:40, one launch (start us, length us, event | category | flops | bytes accessed | tf_op | source)
XLA Modules:
  0.0 150.3 jit_solution(15346572359454794149)
XLA Ops:
  7.2 0.0 reduce-scatter.2.cloned.1.call-start
  7.2 0.0 copy-start.4
  7.2 5.3 %shard_map.75 = (bf16[576,1536]{1,0:T(8,128)(2,1)}, bf16[288,1536]{1,0:T(8,128)(2,1)}, bf16[288,1536]{1,0:T(8,128)(2,1)}) custom-call(bf16[144,256]{1,0:T(8,128)(2,1)} %cot_ref.3, bf16[4,1536,256]{2,1,0:T(8,128)(2,1)} %bitcast.8), custom_call_target="tpu_custom_call" | custom-call | flops 452984832 | bytes 5242880 | tf_op jit(solution)/shard_map/pallas_call | solution.py:45
  12.5 0.0 reduce-scatter.2.cloned.1.call-update
  12.5 3.5 %collective-permute-start.1 = (bf16[288,1536]{1,0:T(8,128)(2,1)}, bf16[288,1536]{1,0:T(8,128)(2,1)S(1)}, u32[]{:S(2)}, u32[]{:S(2)}) collective-permute-start(bf16[288,1536]{1,0:T(8,128)(2,1)} %get-tuple-element.23), channel_id=1, source_target_pairs={{0,12},{12,0},{1,13},{13,1},{2,14},{14,2},{3,15},{15,3},{4,16},{16... | collective-permute-start | bytes 2654216 | tf_op jit(solution)/shard_map/ppermute | solution.py:163
  16.1 0.1 reshape.44
  16.1 39.0 %all_gather.9.own_ref = bf16[288,1536]{1,0:T(8,128)(2,1)S(1)} all-gather(bf16[24,1536]{1,0:T(8,128)(2,1)S(1)} %reshape.44), channel_id=1, replica_groups=mesh['xh'=2,'y'=8,'c'=2,'xl'=2,'z'=12] {'z'}, dimensions={0}, use_global_device_ids=true | all-gather | bytes 958464 | tf_op jit(solution)/shard_map/all_gather | solution.py:171
  55.2 3.0 %collective-permute-start = (bf16[288,1536]{1,0:T(8,128)(2,1)S(1)}, bf16[288,1536]{1,0:T(8,128)(2,1)S(1)}, u32[]{:S(2)}, u32[]{:S(2)}) collective-permute-start(bf16[288,1536]{1,0:T(8,128)(2,1)S(1)} %all_gather.9.own_ref), channel_id=1, source_target_pairs={{0,12},{12,0},{1,13},{13,1},{2,14},{14,2},{3,15},{15,3},{4,16},{16... | collective-permute-start | bytes 2654216 | tf_op jit(solution)/shard_map/ppermute | solution.py:163
  58.1 0.7 shard_map.76
  58.8 11.1 %all_to_all.10 = f32[8,48,128]{2,1,0:T(8,128)S(1)} all-to-all(f32[8,48,128]{2,1,0:T(8,128)S(1)} %shard_map.76), channel_id=1, replica_groups=mesh['xh'=2,'y'=8,'c'=2,'xl'=2,'z'=12] {'y'}, dimensions={0} | all-to-all | bytes 393216 | tf_op jit(solution)/shard_map/all_to_all | solution.py:159
  69.9 4.5 %collective-permute-done.other_ref = bf16[288,1536]{1,0:T(8,128)(2,1)S(1)} collective-permute-done((bf16[288,1536]{1,0:T(8,128)(2,1)S(1)}, bf16[288,1536]{1,0:T(8,128)(2,1)S(1)}, u32[]{:S(2)}, u32[]{:S(2)}) %collective-permute-start) | collective-permute-done | bytes 884768 | tf_op jit(solution)/shard_map/ppermute | solution.py:163
  74.5 0.9 copy-done.1
  75.3 0.7 copy-done.2
  76.1 2.8 %shard_map.77 = (bf16[144,6144]{1,0:T(8,128)(2,1)S(1)}, bf16[16,192,256]{2,1,0:T(8,128)(2,1)S(1)}, bf16[16,192,256]{2,1,0:T(8,128)(2,1)S(1)}) custom-call(bf16[288,1536]{1,0:T(8,128)(2,1)S(1)} %all_gather.9.own_ref, bf16[288,1536]{1,0:T(8,128)(2,1)S(1)} %collective-permute-done.other_ref, bf16[144,256]{1,0:T(8,128)(2,1)S(1)} %copy-done.1, f32[1,6144]{1,0:T(1,128)S(1)} %bitcast.7), custom_call_target="tpu_custom_call" | custom-call | flops 452984832 | bytes 10485760 | tf_op jit(solution)/shard_map/pallas_call | solution.py:142
  78.9 1.9 %collective-permute-start.2 = (bf16[16,192,256]{2,1,0:T(8,128)(2,1)S(1)}, bf16[16,192,256]{2,1,0:T(8,128)(2,1)S(1)}, u32[]{:S(2)}, u32[]{:S(2)}) collective-permute-start(bf16[16,192,256]{2,1,0:T(8,128)(2,1)S(1)} %get-tuple-element.26), channel_id=1, source_target_pairs={{0,24},{24,0},{1,25},{25,1},{2,26},{26,2},{3,27},{27,3},{4,28},{28... | collective-permute-start | bytes 4718600 | tf_op jit(solution)/shard_map/ppermute | solution.py:163
  80.8 2.4 %collective-permute-start.3 = (f32[48,128]{1,0:T(8,128)S(1)}, f32[48,128]{1,0:T(8,128)S(1)}, u32[]{:S(2)}, u32[]{:S(2)}) collective-permute-start(f32[48,128]{1,0:T(8,128)S(1)} %reduce_sum.45), channel_id=1, source_target_pairs={{0,24},{24,0},{1,25},{25,1},{2,26},{26,2},{3,27},{27,3},{4,28},{28... | collective-permute-start | bytes 73736 | tf_op jit(solution)/shard_map/ppermute | solution.py:163
  83.3 3.2 %convolution_convert_fusion = bf16[144,256]{1,0:T(8,128)(2,1)} fusion(bf16[144,6144]{1,0:T(8,128)(2,1)S(1)} %get-tuple-element.28, bf16[6144,256]{1,0:T(8,128)(2,1)} %param.6), kind=kOutput, calls=%fused_computation.1 | convolution fusion | flops 453021696 | bytes 4988928 | tf_op jit(solution)/shard_map/dot_general | solution.py:180
  86.4 1.7 %add.25 = bf16[16,192,256]{2,1,0:T(8,128)(2,1)} add(bf16[16,192,256]{2,1,0:T(8,128)(2,1)S(1)} %get-tuple-element.25, bf16[16,192,256]{2,1,0:T(8,128)(2,1)S(1)} %collective-permute-done.2) | non-fusion elementwise | flops 786432 | bytes 4718592 | tf_op jit(solution)/shard_map/add | solution.py:179
  88.1 9.8 %all-to-all-start.1 = ((bf16[16,192,256]{2,1,0:T(8,128)(2,1)}), bf16[16,192,256]{2,1,0:T(8,128)(2,1)S(1)}, u32[]{:S(2)}, u32[]{:S(2)}) async-start(bf16[16,192,256]{2,1,0:T(8,128)(2,1)} %add.25), calls=%async_computation.2 | async-start | bytes 3145728 | tf_op jit(solution)/shard_map/all_to_all | solution.py:159
  97.9 0.2 fusion.6
  98.1 21.2 %all-gather = f32[576,128]{1,0:T(8,128)S(1)} all-gather(f32[48,128]{1,0:T(8,128)S(1)} %add.26), channel_id=2, replica_groups=mesh['xh'=2,'y'=8,'c'=2,'xl'=2,'z'=12] {'z'}, dimensions={0}, use_global_device_ids=true | all-gather | bytes 319488 | tf_op jit(solution)/shard_map/all_gather | solution.py:186
  119.3 3.0 %collective-permute-start.5 = (f32[48,128]{1,0:T(8,128)S(1)}, f32[48,128]{1,0:T(8,128)S(1)}, u32[]{:S(2)}, u32[]{:S(2)}) collective-permute-start(f32[48,128]{1,0:T(8,128)S(1)} %reduce_sum.47), channel_id=1, source_target_pairs={{0,12},{12,0},{1,13},{13,1},{2,14},{14,2},{3,15},{15,3},{4,16},{16... | collective-permute-start | bytes 73736 | tf_op jit(solution)/shard_map/ppermute | solution.py:163
  122.2 7.8 %collective-permute-done.5 = f32[48,128]{1,0:T(8,128)S(1)} collective-permute-done((f32[48,128]{1,0:T(8,128)S(1)}, f32[48,128]{1,0:T(8,128)S(1)}, u32[]{:S(2)}, u32[]{:S(2)}) %collective-permute-start.5) | collective-permute-done | bytes 24608 | tf_op jit(solution)/shard_map/ppermute | solution.py:163
  130.0 5.0 %collective-permute-start.6 = (f32[48,128]{1,0:T(8,128)S(1)}, f32[48,128]{1,0:T(8,128)S(1)}, u32[]{:S(2)}, u32[]{:S(2)}) collective-permute-start(f32[48,128]{1,0:T(8,128)S(1)} %add.29), channel_id=1, source_target_pairs={{0,384},{384,0},{1,385},{385,1},{2,386},{386,2},{3,387},{387,3},{4... | collective-permute-start | bytes 73736 | tf_op jit(solution)/shard_map/ppermute | solution.py:163
  135.0 0.1 select_n.19
  135.1 2.3 %collective-permute-start.4 = (bf16[6,6144]{1,0:T(8,128)(2,1)S(1)}, bf16[6,6144]{1,0:T(8,128)(2,1)S(1)}, u32[]{:S(2)}, u32[]{:S(2)}) collective-permute-start(bf16[6,6144]{1,0:T(8,128)(2,1)S(1)} %select_n.19), channel_id=1, source_target_pairs={{0,12},{12,0},{1,13},{13,1},{2,14},{14,2},{3,15},{15,3},{4,16},{16... | collective-permute-start | bytes 221192 | tf_op jit(solution)/shard_map/ppermute | solution.py:163
  137.4 0.1 reshape.48
  137.5 0.6 add_bitcast_fusion
  138.1 3.5 %collective-permute-done.4 = bf16[6,6144]{1,0:T(8,128)(2,1)S(1)} collective-permute-done((bf16[6,6144]{1,0:T(8,128)(2,1)S(1)}, bf16[6,6144]{1,0:T(8,128)(2,1)S(1)}, u32[]{:S(2)}, u32[]{:S(2)}) %collective-permute-start.4) | collective-permute-done | bytes 73760 | tf_op jit(solution)/shard_map/ppermute | solution.py:163
  141.6 0.2 fusion.2
  141.8 0.7 fusion.5
  142.6 0.9 convert_reduce_fusion
  (24 shorter events, 0.1 us)
Async XLA Ops:
  7.2 80.9 %reduce-scatter.2.cloned.1.call-start = ((), (), s32[]{:S(2)}) async-start(), calls=%async_computation.3 | async-start | bytes 1916928 | tf_op jit(solution)/shard_map/reduce_scatter | solution.py:168
  7.2 8.9 %copy-start.4 = (bf16[6,6144]{1,0:T(8,128)(2,1)S(1)}, bf16[6,6144]{1,0:T(8,128)(2,1)}, u32[]{:S(2)}) copy-start(bf16[6,6144]{1,0:T(8,128)(2,1)} %param.4) | copy-start | bytes 221188
  12.5 45.6 %copy-start = (bf16[288,1536]{1,0:T(8,128)(2,1)S(1)}, bf16[288,1536]{1,0:T(8,128)(2,1)}, u32[]{:S(2)}) copy-start(bf16[288,1536]{1,0:T(8,128)(2,1)} %get-tuple-element.22.keep_ref) | copy-start | bytes 2654212
  12.5 45.6 %collective-permute-start.1 = (bf16[288,1536]{1,0:T(8,128)(2,1)}, bf16[288,1536]{1,0:T(8,128)(2,1)S(1)}, u32[]{:S(2)}, u32[]{:S(2)}) collective-permute-start(bf16[288,1536]{1,0:T(8,128)(2,1)} %get-tuple-element.23), channel_id=1, source_target_pairs={{0,12},{12,0},{1,13},{13,1},{2,14},{14,2},{3,15},{15,3},{4,16},{16... | collective-permute-start | bytes 2654216 | tf_op jit(solution)/shard_map/ppermute | solution.py:163
  55.2 19.3 %collective-permute-start = (bf16[288,1536]{1,0:T(8,128)(2,1)S(1)}, bf16[288,1536]{1,0:T(8,128)(2,1)S(1)}, u32[]{:S(2)}, u32[]{:S(2)}) collective-permute-start(bf16[288,1536]{1,0:T(8,128)(2,1)S(1)} %all_gather.9.own_ref), channel_id=1, source_target_pairs={{0,12},{12,0},{1,13},{13,1},{2,14},{14,2},{3,15},{15,3},{4,16},{16... | collective-permute-start | bytes 2654216 | tf_op jit(solution)/shard_map/ppermute | solution.py:163
  74.5 0.9 copy-start.1
  75.3 0.7 copy-start.2
  78.9 7.5 %collective-permute-start.2 = (bf16[16,192,256]{2,1,0:T(8,128)(2,1)S(1)}, bf16[16,192,256]{2,1,0:T(8,128)(2,1)S(1)}, u32[]{:S(2)}, u32[]{:S(2)}) collective-permute-start(bf16[16,192,256]{2,1,0:T(8,128)(2,1)S(1)} %get-tuple-element.26), channel_id=1, source_target_pairs={{0,24},{24,0},{1,25},{25,1},{2,26},{26,2},{3,27},{27,3},{4,28},{28... | collective-permute-start | bytes 4718600 | tf_op jit(solution)/shard_map/ppermute | solution.py:163
  80.8 5.6 %collective-permute-start.3 = (f32[48,128]{1,0:T(8,128)S(1)}, f32[48,128]{1,0:T(8,128)S(1)}, u32[]{:S(2)}, u32[]{:S(2)}) collective-permute-start(f32[48,128]{1,0:T(8,128)S(1)} %reduce_sum.45), channel_id=1, source_target_pairs={{0,24},{24,0},{1,25},{25,1},{2,26},{26,2},{3,27},{27,3},{4,28},{28... | collective-permute-start | bytes 73736 | tf_op jit(solution)/shard_map/ppermute | solution.py:163
  88.1 9.8 %copy-start.5 = (bf16[6,6144]{1,0:T(8,128)(2,1)S(1)}, bf16[6,6144]{1,0:T(8,128)(2,1)}, u32[]{:S(2)}) copy-start(bf16[6,6144]{1,0:T(8,128)(2,1)} %param.4) | copy-start | bytes 221188
  88.1 53.5 %copy-start.3 = (f32[6144]{0:T(1024)S(1)}, f32[6144]{0:T(1024)}, u32[]{:S(2)}) copy-start(f32[6144]{0:T(1024)} %param.5) | copy-start | bytes 73732
  88.1 46.9 %copy-start.6 = (bf16[48,1536]{1,0:T(8,128)(2,1)S(1)}, bf16[48,1536]{1,0:T(8,128)(2,1)}, u32[]{:S(2)}) copy-start(bf16[48,1536]{1,0:T(8,128)(2,1)} %reduce-scatter.2.cloned.1.call-done) | copy-start | bytes 442372
  88.1 54.5 %all-to-all-start.1 = ((bf16[16,192,256]{2,1,0:T(8,128)(2,1)}), bf16[16,192,256]{2,1,0:T(8,128)(2,1)S(1)}, u32[]{:S(2)}, u32[]{:S(2)}) async-start(bf16[16,192,256]{2,1,0:T(8,128)(2,1)} %add.25), calls=%async_computation.2 | async-start | bytes 3145728 | tf_op jit(solution)/shard_map/all_to_all | solution.py:159
  119.3 10.8 %collective-permute-start.5 = (f32[48,128]{1,0:T(8,128)S(1)}, f32[48,128]{1,0:T(8,128)S(1)}, u32[]{:S(2)}, u32[]{:S(2)}) collective-permute-start(f32[48,128]{1,0:T(8,128)S(1)} %reduce_sum.47), channel_id=1, source_target_pairs={{0,12},{12,0},{1,13},{13,1},{2,14},{14,2},{3,15},{15,3},{4,16},{16... | collective-permute-start | bytes 73736 | tf_op jit(solution)/shard_map/ppermute | solution.py:163
  130.0 7.5 %collective-permute-start.6 = (f32[48,128]{1,0:T(8,128)S(1)}, f32[48,128]{1,0:T(8,128)S(1)}, u32[]{:S(2)}, u32[]{:S(2)}) collective-permute-start(f32[48,128]{1,0:T(8,128)S(1)} %add.29), channel_id=1, source_target_pairs={{0,384},{384,0},{1,385},{385,1},{2,386},{386,2},{3,387},{387,3},{4... | collective-permute-start | bytes 73736 | tf_op jit(solution)/shard_map/ppermute | solution.py:163
  135.1 6.5 %collective-permute-start.4 = (bf16[6,6144]{1,0:T(8,128)(2,1)S(1)}, bf16[6,6144]{1,0:T(8,128)(2,1)S(1)}, u32[]{:S(2)}, u32[]{:S(2)}) collective-permute-start(bf16[6,6144]{1,0:T(8,128)(2,1)S(1)} %select_n.19), channel_id=1, source_target_pairs={{0,12},{12,0},{1,13},{13,1},{2,14},{14,2},{3,15},{15,3},{4,16},{16... | collective-permute-start | bytes 221192 | tf_op jit(solution)/shard_map/ppermute | solution.py:163
Sparse Core Ops, SparseCore 0:
  12.6 67.6 reduce-scatter.1

commit v5 on v4

--- a/solution.py
+++ b/solution.py
@@ -174,7 +174,7 @@
     part = gain_terms(own, grad_keep, grad_got)
     part = jnp.sum(exchange(part, "y"), axis=0)
     other, part = lax.optimization_barrier((other, part))
-    part = part + swap(part, "c")
+    part = part + swap(part, "xh")
     restored, keep, send = main_products(own, other, cotangent, norm_gain.reshape(1, D))
     share = keep + swap(send, "c")
     projected = jnp.dot(restored, proj_weight, preferred_element_type=jnp.float32)
@@ -186,7 +186,7 @@
     part = jnp.sum(lax.all_gather(part, "z"), axis=0)
     part, grad_rows = lax.optimization_barrier((part, grad_rows))
     part = part + swap(part, "xl")
-    gain_grad = (part + swap(part, "xh")).reshape(D)
+    gain_grad = (part + swap(part, "c")).reshape(D)
 
     values = tokens.astype(jnp.float32)
     rsq = lax.rsqrt(jnp.mean(values * values, axis=-1, keepdims=True) + 1e-05)

time: 151 us -> 149 us (0.987)
  the two profiles are of different devices: /device:TPU:40 before, /device:TPU:44 now
where the time goes in v5:
time: 149 us; the launch traced here: 148 us
  blocking collectives  71.6 us (48%)
  starting transfers between devices  27.3 us (18%)
  waiting for transfers between devices  17 us (11%)
  between operations  14.2 us (10%)
  Pallas kernels  8.76 us (6%)
  other arithmetic  4.4 us (3%)
  matrix products  3.16 us (2%)
  local copies, waits for them, and re-layouts  1.82 us (1%)
    all_gather x1, blocking collectives, body(): own = lax.all_gather(chunk, 'z', axis=0, tiled=True)  39.1 us
    all_gather x1, blocking collectives, body(): part = jnp.sum(lax.all_gather(part, 'z'), axis=0)  21.2 us
    ppermute x7, starting transfers between devices, swap(): return lax.ppermute(array, axis, [(0, 1), (1, 0)])  18 us
    ppermute x7, waiting for transfers between devices, swap(): return lax.ppermute(array, axis, [(0, 1), (1, 0)])  17 us
    all_to_all x1, blocking collectives, exchange(): return lax.all_to_all(array, axes, 0, 0, tiled=True)  11.3 us
    all_to_all x1, starting transfers between devices, exchange(): return lax.all_to_all(array, axes, 0, 0, tiled=True)  9.26 us
    pallas_call x1, Pallas kernels, grad_terms(): pl.pallas_call(grad_kernel, grid=(FQ // BLOCK,), out_shape=(jax.ShapeDtyp...  5.27 us
    dot_general x1, matrix products, body(): jnp.dot(restored, proj_weight, preferred_element_type=jnp.float32)  3.16 us
  transfers between devices with their start and end apart: 9, of which 4 were waited for; matrix products, arithmetic and copies ran while one was open for 5% of the time, Pallas kernels for 2%

profile of v5, /device:TPU:44, one launch (start us, length us, event | category | flops | bytes accessed | tf_op | source)
XLA Modules:
  0.0 148.2 jit_solution(1218068278525806248)
XLA Ops:
  7.2 0.0 reduce-scatter.2.cloned.1.call-start
  7.2 5.3 %shard_map.75 = (bf16[576,1536]{1,0:T(8,128)(2,1)}, bf16[288,1536]{1,0:T(8,128)(2,1)}, bf16[288,1536]{1,0:T(8,128)(2,1)}) custom-call(bf16[144,256]{1,0:T(8,128)(2,1)} %cot_ref.3, bf16[4,1536,256]{2,1,0:T(8,128)(2,1)} %bitcast.8), custom_call_target="tpu_custom_call" | custom-call | flops 452984832 | bytes 5242880 | tf_op jit(solution)/shard_map/pallas_call | solution.py:45
  12.5 0.0 reduce-scatter.2.cloned.1.call-update
  12.5 3.2 %collective-permute-start.1 = (bf16[288,1536]{1,0:T(8,128)(2,1)}, bf16[288,1536]{1,0:T(8,128)(2,1)S(1)}, u32[]{:S(2)}, u32[]{:S(2)}) collective-permute-start(bf16[288,1536]{1,0:T(8,128)(2,1)} %get-tuple-element.23), channel_id=1, source_target_pairs={{0,12},{12,0},{1,13},{13,1},{2,14},{14,2},{3,15},{15,3},{4,16},{16... | collective-permute-start | bytes 2654216 | tf_op jit(solution)/shard_map/ppermute | solution.py:163
  15.8 0.1 reshape.44
  15.8 39.1 %all_gather.9.own_ref = bf16[288,1536]{1,0:T(8,128)(2,1)S(1)} all-gather(bf16[24,1536]{1,0:T(8,128)(2,1)S(1)} %reshape.44), channel_id=1, replica_groups=mesh['xh'=2,'y'=8,'c'=2,'xl'=2,'z'=12] {'z'}, dimensions={0}, use_global_device_ids=true | all-gather | bytes 958464 | tf_op jit(solution)/shard_map/all_gather | solution.py:171
  55.0 3.2 %collective-permute-start = (bf16[288,1536]{1,0:T(8,128)(2,1)S(1)}, bf16[288,1536]{1,0:T(8,128)(2,1)S(1)}, u32[]{:S(2)}, u32[]{:S(2)}) collective-permute-start(bf16[288,1536]{1,0:T(8,128)(2,1)S(1)} %all_gather.9.own_ref), channel_id=1, source_target_pairs={{0,12},{12,0},{1,13},{13,1},{2,14},{14,2},{3,15},{15,3},{4,16},{16... | collective-permute-start | bytes 2654216 | tf_op jit(solution)/shard_map/ppermute | solution.py:163
  58.1 0.7 shard_map.76
  58.8 11.3 %all_to_all.10 = f32[8,48,128]{2,1,0:T(8,128)S(1)} all-to-all(f32[8,48,128]{2,1,0:T(8,128)S(1)} %shard_map.76), channel_id=1, replica_groups=mesh['xh'=2,'y'=8,'c'=2,'xl'=2,'z'=12] {'y'}, dimensions={0} | all-to-all | bytes 393216 | tf_op jit(solution)/shard_map/all_to_all | solution.py:159
  70.1 4.8 %collective-permute-done.other_ref = bf16[288,1536]{1,0:T(8,128)(2,1)S(1)} collective-permute-done((bf16[288,1536]{1,0:T(8,128)(2,1)S(1)}, bf16[288,1536]{1,0:T(8,128)(2,1)S(1)}, u32[]{:S(2)}, u32[]{:S(2)}) %collective-permute-start) | collective-permute-done | bytes 884768 | tf_op jit(solution)/shard_map/ppermute | solution.py:163
  74.9 0.9 copy-done.1
  75.8 0.7 copy-done.2
  76.5 2.8 %shard_map.77 = (bf16[144,6144]{1,0:T(8,128)(2,1)S(1)}, bf16[16,192,256]{2,1,0:T(8,128)(2,1)S(1)}, bf16[16,192,256]{2,1,0:T(8,128)(2,1)S(1)}) custom-call(bf16[288,1536]{1,0:T(8,128)(2,1)S(1)} %all_gather.9.own_ref, bf16[288,1536]{1,0:T(8,128)(2,1)S(1)} %collective-permute-done.other_ref, bf16[144,256]{1,0:T(8,128)(2,1)S(1)} %copy-done.1, f32[1,6144]{1,0:T(1,128)S(1)} %bitcast.7), custom_call_target="tpu_custom_call" | custom-call | flops 452984832 | bytes 10485760 | tf_op jit(solution)/shard_map/pallas_call | solution.py:142
  79.4 1.9 %collective-permute-start.2 = (bf16[16,192,256]{2,1,0:T(8,128)(2,1)S(1)}, bf16[16,192,256]{2,1,0:T(8,128)(2,1)S(1)}, u32[]{:S(2)}, u32[]{:S(2)}) collective-permute-start(bf16[16,192,256]{2,1,0:T(8,128)(2,1)S(1)} %get-tuple-element.26), channel_id=1, source_target_pairs={{0,24},{24,0},{1,25},{25,1},{2,26},{26,2},{3,27},{27,3},{4,28},{28... | collective-permute-start | bytes 4718600 | tf_op jit(solution)/shard_map/ppermute | solution.py:163
  81.3 2.0 %collective-permute-start.3 = (f32[48,128]{1,0:T(8,128)S(1)}, f32[48,128]{1,0:T(8,128)S(1)}, u32[]{:S(2)}, u32[]{:S(2)}) collective-permute-start(f32[48,128]{1,0:T(8,128)S(1)} %reduce_sum.45), channel_id=1, source_target_pairs={{0,384},{384,0},{1,385},{385,1},{2,386},{386,2},{3,387},{387,3},{4... | collective-permute-start | bytes 73736 | tf_op jit(solution)/shard_map/ppermute | solution.py:163
  83.3 3.2 %convolution_convert_fusion = bf16[144,256]{1,0:T(8,128)(2,1)} fusion(bf16[144,6144]{1,0:T(8,128)(2,1)S(1)} %get-tuple-element.28, bf16[6144,256]{1,0:T(8,128)(2,1)} %param.6), kind=kOutput, calls=%fused_computation.1 | convolution fusion | flops 453021696 | bytes 4988928 | tf_op jit(solution)/shard_map/dot_general | solution.py:180
  86.4 2.1 %collective-permute-done.3 = f32[48,128]{1,0:T(8,128)S(1)} collective-permute-done((f32[48,128]{1,0:T(8,128)S(1)}, f32[48,128]{1,0:T(8,128)S(1)}, u32[]{:S(2)}, u32[]{:S(2)}) %collective-permute-start.3) | collective-permute-done | bytes 24608 | tf_op jit(solution)/shard_map/ppermute | solution.py:163
  88.5 1.7 %add.25 = bf16[16,192,256]{2,1,0:T(8,128)(2,1)} add(bf16[16,192,256]{2,1,0:T(8,128)(2,1)S(1)} %get-tuple-element.25, bf16[16,192,256]{2,1,0:T(8,128)(2,1)S(1)} %collective-permute-done.2) | non-fusion elementwise | flops 786432 | bytes 4718592 | tf_op jit(solution)/shard_map/add | solution.py:179
  90.2 9.3 %all-to-all-start.1 = ((bf16[16,192,256]{2,1,0:T(8,128)(2,1)}), bf16[16,192,256]{2,1,0:T(8,128)(2,1)S(1)}, u32[]{:S(2)}, u32[]{:S(2)}) async-start(bf16[16,192,256]{2,1,0:T(8,128)(2,1)} %add.25), calls=%async_computation.2 | async-start | bytes 3145728 | tf_op jit(solution)/shard_map/all_to_all | solution.py:159
  99.5 0.2 fusion.6
  99.6 21.2 %all-gather = f32[576,128]{1,0:T(8,128)S(1)} all-gather(f32[48,128]{1,0:T(8,128)S(1)} %add.26), channel_id=2, replica_groups=mesh['xh'=2,'y'=8,'c'=2,'xl'=2,'z'=12] {'z'}, dimensions={0}, use_global_device_ids=true | all-gather | bytes 319488 | tf_op jit(solution)/shard_map/all_gather | solution.py:186
  120.8 3.6 %collective-permute-start.5 = (f32[48,128]{1,0:T(8,128)S(1)}, f32[48,128]{1,0:T(8,128)S(1)}, u32[]{:S(2)}, u32[]{:S(2)}) collective-permute-start(f32[48,128]{1,0:T(8,128)S(1)} %reduce_sum.47), channel_id=1, source_target_pairs={{0,12},{12,0},{1,13},{13,1},{2,14},{14,2},{3,15},{15,3},{4,16},{16... | collective-permute-start | bytes 73736 | tf_op jit(solution)/shard_map/ppermute | solution.py:163
  124.4 6.0 %collective-permute-done.5 = f32[48,128]{1,0:T(8,128)S(1)} collective-permute-done((f32[48,128]{1,0:T(8,128)S(1)}, f32[48,128]{1,0:T(8,128)S(1)}, u32[]{:S(2)}, u32[]{:S(2)}) %collective-permute-start.5) | collective-permute-done | bytes 24608 | tf_op jit(solution)/shard_map/ppermute | solution.py:163
  130.4 1.9 %collective-permute-start.6 = (f32[48,128]{1,0:T(8,128)S(1)}, f32[48,128]{1,0:T(8,128)S(1)}, u32[]{:S(2)}, u32[]{:S(2)}) collective-permute-start(f32[48,128]{1,0:T(8,128)S(1)} %add.29), channel_id=1, source_target_pairs={{0,24},{24,0},{1,25},{25,1},{2,26},{26,2},{3,27},{27,3},{4,28},{28... | collective-permute-start | bytes 73736 | tf_op jit(solution)/shard_map/ppermute | solution.py:163
  132.4 0.1 select_n.19
  132.4 2.3 %collective-permute-start.4 = (bf16[6,6144]{1,0:T(8,128)(2,1)S(1)}, bf16[6,6144]{1,0:T(8,128)(2,1)S(1)}, u32[]{:S(2)}, u32[]{:S(2)}) collective-permute-start(bf16[6,6144]{1,0:T(8,128)(2,1)S(1)} %select_n.19), channel_id=1, source_target_pairs={{0,12},{12,0},{1,13},{13,1},{2,14},{14,2},{3,15},{15,3},{4,16},{16... | collective-permute-start | bytes 221192 | tf_op jit(solution)/shard_map/ppermute | solution.py:163
  134.7 0.1 reshape.48
  134.8 0.6 add_bitcast_fusion
  135.4 4.1 %collective-permute-done.4 = bf16[6,6144]{1,0:T(8,128)(2,1)S(1)} collective-permute-done((bf16[6,6144]{1,0:T(8,128)(2,1)S(1)}, bf16[6,6144]{1,0:T(8,128)(2,1)S(1)}, u32[]{:S(2)}, u32[]{:S(2)}) %collective-permute-start.4) | collective-permute-done | bytes 73760 | tf_op jit(solution)/shard_map/ppermute | solution.py:163
  139.5 0.2 fusion.2
  139.8 0.7 fusion.5
  140.5 0.9 convert_reduce_fusion
  (24 shorter events, 0.1 us)
Async XLA Ops:
  7.2 83.0 %reduce-scatter.2.cloned.1.call-start = ((), (), s32[]{:S(2)}) async-start(), calls=%async_computation.3 | async-start | bytes 1916928 | tf_op jit(solution)/shard_map/reduce_scatter | solution.py:168
  7.2 8.6 %copy-start.4 = (bf16[6,6144]{1,0:T(8,128)(2,1)S(1)}, bf16[6,6144]{1,0:T(8,128)(2,1)}, u32[]{:S(2)}) copy-start(bf16[6,6144]{1,0:T(8,128)(2,1)} %param.4) | copy-start | bytes 221188
  12.5 45.6 %copy-start = (bf16[288,1536]{1,0:T(8,128)(2,1)S(1)}, bf16[288,1536]{1,0:T(8,128)(2,1)}, u32[]{:S(2)}) copy-start(bf16[288,1536]{1,0:T(8,128)(2,1)} %get-tuple-element.22.keep_ref) | copy-start | bytes 2654212
  12.5 45.6 %collective-permute-start.1 = (bf16[288,1536]{1,0:T(8,128)(2,1)}, bf16[288,1536]{1,0:T(8,128)(2,1)S(1)}, u32[]{:S(2)}, u32[]{:S(2)}) collective-permute-start(bf16[288,1536]{1,0:T(8,128)(2,1)} %get-tuple-element.23), channel_id=1, source_target_pairs={{0,12},{12,0},{1,13},{13,1},{2,14},{14,2},{3,15},{15,3},{4,16},{16... | collective-permute-start | bytes 2654216 | tf_op jit(solution)/shard_map/ppermute | solution.py:163
  55.0 20.0 %collective-permute-start = (bf16[288,1536]{1,0:T(8,128)(2,1)S(1)}, bf16[288,1536]{1,0:T(8,128)(2,1)S(1)}, u32[]{:S(2)}, u32[]{:S(2)}) collective-permute-start(bf16[288,1536]{1,0:T(8,128)(2,1)S(1)} %all_gather.9.own_ref), channel_id=1, source_target_pairs={{0,12},{12,0},{1,13},{13,1},{2,14},{14,2},{3,15},{15,3},{4,16},{16... | collective-permute-start | bytes 2654216 | tf_op jit(solution)/shard_map/ppermute | solution.py:163
  74.9 0.9 copy-start.1
  75.8 0.7 copy-start.2
  79.4 9.2 %collective-permute-start.2 = (bf16[16,192,256]{2,1,0:T(8,128)(2,1)S(1)}, bf16[16,192,256]{2,1,0:T(8,128)(2,1)S(1)}, u32[]{:S(2)}, u32[]{:S(2)}) collective-permute-start(bf16[16,192,256]{2,1,0:T(8,128)(2,1)S(1)} %get-tuple-element.26), channel_id=1, source_target_pairs={{0,24},{24,0},{1,25},{25,1},{2,26},{26,2},{3,27},{27,3},{4,28},{28... | collective-permute-start | bytes 4718600 | tf_op jit(solution)/shard_map/ppermute | solution.py:163
  81.3 7.2 %collective-permute-start.3 = (f32[48,128]{1,0:T(8,128)S(1)}, f32[48,128]{1,0:T(8,128)S(1)}, u32[]{:S(2)}, u32[]{:S(2)}) collective-permute-start(f32[48,128]{1,0:T(8,128)S(1)} %reduce_sum.45), channel_id=1, source_target_pairs={{0,384},{384,0},{1,385},{385,1},{2,386},{386,2},{3,387},{387,3},{4... | collective-permute-start | bytes 73736 | tf_op jit(solution)/shard_map/ppermute | solution.py:163
  90.2 9.3 %copy-start.5 = (bf16[6,6144]{1,0:T(8,128)(2,1)S(1)}, bf16[6,6144]{1,0:T(8,128)(2,1)}, u32[]{:S(2)}) copy-start(bf16[6,6144]{1,0:T(8,128)(2,1)} %param.4) | copy-start | bytes 221188
  90.2 49.3 %copy-start.3 = (f32[6144]{0:T(1024)S(1)}, f32[6144]{0:T(1024)}, u32[]{:S(2)}) copy-start(f32[6144]{0:T(1024)} %param.5) | copy-start | bytes 73732
  90.2 42.1 %copy-start.6 = (bf16[48,1536]{1,0:T(8,128)(2,1)S(1)}, bf16[48,1536]{1,0:T(8,128)(2,1)}, u32[]{:S(2)}) copy-start(bf16[48,1536]{1,0:T(8,128)(2,1)} %reduce-scatter.2.cloned.1.call-done) | copy-start | bytes 442372
  90.2 50.3 %all-to-all-start.1 = ((bf16[16,192,256]{2,1,0:T(8,128)(2,1)}), bf16[16,192,256]{2,1,0:T(8,128)(2,1)S(1)}, u32[]{:S(2)}, u32[]{:S(2)}) async-start(bf16[16,192,256]{2,1,0:T(8,128)(2,1)} %add.25), calls=%async_computation.2 | async-start | bytes 3145728 | tf_op jit(solution)/shard_map/all_to_all | solution.py:159
  120.8 9.6 %collective-permute-start.5 = (f32[48,128]{1,0:T(8,128)S(1)}, f32[48,128]{1,0:T(8,128)S(1)}, u32[]{:S(2)}, u32[]{:S(2)}) collective-permute-start(f32[48,128]{1,0:T(8,128)S(1)} %reduce_sum.47), channel_id=1, source_target_pairs={{0,12},{12,0},{1,13},{13,1},{2,14},{14,2},{3,15},{15,3},{4,16},{16... | collective-permute-start | bytes 73736 | tf_op jit(solution)/shard_map/ppermute | solution.py:163
  130.4 4.4 %collective-permute-start.6 = (f32[48,128]{1,0:T(8,128)S(1)}, f32[48,128]{1,0:T(8,128)S(1)}, u32[]{:S(2)}, u32[]{:S(2)}) collective-permute-start(f32[48,128]{1,0:T(8,128)S(1)} %add.29), channel_id=1, source_target_pairs={{0,24},{24,0},{1,25},{25,1},{2,26},{26,2},{3,27},{27,3},{4,28},{28... | collective-permute-start | bytes 73736 | tf_op jit(solution)/shard_map/ppermute | solution.py:163
  132.4 7.1 %collective-permute-start.4 = (bf16[6,6144]{1,0:T(8,128)(2,1)S(1)}, bf16[6,6144]{1,0:T(8,128)(2,1)S(1)}, u32[]{:S(2)}, u32[]{:S(2)}) collective-permute-start(bf16[6,6144]{1,0:T(8,128)(2,1)S(1)} %select_n.19), channel_id=1, source_target_pairs={{0,12},{12,0},{1,13},{13,1},{2,14},{14,2},{3,15},{15,3},{4,16},{16... | collective-permute-start | bytes 221192 | tf_op jit(solution)/shard_map/ppermute | solution.py:163
Sparse Core Ops, SparseCore 0:
  12.6 68.2 reduce-scatter.1

commit v6 on v5

--- a/solution.py
+++ b/solution.py
@@ -15,6 +15,7 @@
 HALF = ROWS // 2
 CHUNK = TOK * Q
 BLOCK = 384
+STEP = 256
 OWNED = BLOCK // 2
 NT = (((1,), (1,)), ((), ()))
 TN = (((0,), (0,)), ((), ()))
@@ -29,9 +30,9 @@
     theirs = pl.multiple_of((1 - side) * HALF, HALF)
     for q in range(Q):
         part = lax.dot_general(cot_ref[...], w_ref[q], NT, preferred_element_type=jnp.float32)
-        for b in range(BLOCK // 128):
+        for b in range(STEP // 128):
             wide[b, pl.ds(q, GROUP, stride=Q), :] = part[:, b * 128 : (b + 1) * 128]
-    for b in range(BLOCK // 128):
+    for b in range(STEP // 128):
         lanes = slice(b * 128, (b + 1) * 128)
         keep_ref[:, lanes] = wide[b, pl.ds(mine, HALF), :].astype(jnp.bfloat16)
         send_ref[:, lanes] = wide[b, pl.ds(theirs, HALF), :].astype(jnp.bfloat16)
@@ -44,18 +45,18 @@
     half = jax.ShapeDtypeStruct((HALF, FQ), jnp.bfloat16)
     return pl.pallas_call(
         grad_kernel,
-        grid=(FQ // BLOCK,),
+        grid=(FQ // STEP,),
         out_shape=(jax.ShapeDtypeStruct((ROWS, FQ), jnp.bfloat16), half, half),
         in_specs=[
             pl.BlockSpec((GROUP, COLS), lambda i: (0, 0)),
-            pl.BlockSpec((Q, BLOCK, COLS), lambda i: (0, i, 0)),
+            pl.BlockSpec((Q, STEP, COLS), lambda i: (0, i, 0)),
         ],
         out_specs=(
-            pl.BlockSpec((ROWS, BLOCK), lambda i: (0, i)),
-            pl.BlockSpec((HALF, BLOCK), lambda i: (0, i)),
-            pl.BlockSpec((HALF, BLOCK), lambda i: (0, i)),
+            pl.BlockSpec((ROWS, STEP), lambda i: (0, i)),
+            pl.BlockSpec((HALF, STEP), lambda i: (0, i)),
+            pl.BlockSpec((HALF, STEP), lambda i: (0, i)),
         ),
-        scratch_shapes=[pltpu.VMEM((BLOCK // 128, ROWS, 128), jnp.float32)],
+        scratch_shapes=[pltpu.VMEM((STEP // 128, ROWS, 128), jnp.float32)],
         compiler_params=STREAMED,
         cost_estimate=pl.CostEstimate(
             flops=2 * GROUP * D * COLS, bytes_accessed=5 * 2**20, transcendentals=0

time: 149 us -> 150 us (level)
  no operation moved by 1% of the time
where the time goes in v6:
time: 150 us; the launch traced here: 149 us
  blocking collectives  71.7 us (48%)
  starting transfers between devices  27.3 us (18%)
  waiting for transfers between devices  16.9 us (11%)
  between operations  14.2 us (9%)
  Pallas kernels  9.92 us (7%)
  other arithmetic  4.4 us (3%)
  matrix products  3.16 us (2%)
  local copies, waits for them, and re-layouts  1.82 us (1%)
    all_gather x1, blocking collectives, body(): own = lax.all_gather(chunk, 'z', axis=0, tiled=True)  39.1 us
    all_gather x1, blocking collectives, body(): part = jnp.sum(lax.all_gather(part, 'z'), axis=0)  21.2 us
    ppermute x7, starting transfers between devices, swap(): return lax.ppermute(array, axis, [(0, 1), (1, 0)])  18.1 us
    ppermute x7, waiting for transfers between devices, swap(): return lax.ppermute(array, axis, [(0, 1), (1, 0)])  16.8 us
    all_to_all x1, blocking collectives, exchange(): return lax.all_to_all(array, axes, 0, 0, tiled=True)  11.4 us
    all_to_all x1, starting transfers between devices, exchange(): return lax.all_to_all(array, axes, 0, 0, tiled=True)  9.25 us
    pallas_call x1, Pallas kernels, grad_terms(): pl.pallas_call(grad_kernel, grid=(FQ // STEP,), out_shape=(jax.ShapeDtype...  6.43 us
    dot_general x1, matrix products, body(): jnp.dot(restored, proj_weight, preferred_element_type=jnp.float32)  3.16 us
  transfers between devices with their start and end apart: 9, of which 4 were waited for; matrix products, arithmetic and copies ran while one was open for 5% of the time, Pallas kernels for 2%

profile of v6, /device:TPU:44, one launch (start us, length us, event | category | flops | bytes accessed | tf_op | source)
XLA Modules:
  0.0 149.4 jit_solution(17108025450952525627)
XLA Ops:
  7.2 0.0 reduce-scatter.2.cloned.1.call-start
  7.2 6.4 %shard_map.75 = (bf16[576,1536]{1,0:T(8,128)(2,1)}, bf16[288,1536]{1,0:T(8,128)(2,1)}, bf16[288,1536]{1,0:T(8,128)(2,1)}) custom-call(bf16[144,256]{1,0:T(8,128)(2,1)} %cot_ref.3, bf16[4,1536,256]{2,1,0:T(8,128)(2,1)} %bitcast.8), custom_call_target="tpu_custom_call" | custom-call | flops 452984832 | bytes 5242880 | tf_op jit(solution)/shard_map/pallas_call | solution.py:46
  13.7 0.0 reduce-scatter.2.cloned.1.call-update
  13.7 3.2 %collective-permute-start.1 = (bf16[288,1536]{1,0:T(8,128)(2,1)}, bf16[288,1536]{1,0:T(8,128)(2,1)S(1)}, u32[]{:S(2)}, u32[]{:S(2)}) collective-permute-start(bf16[288,1536]{1,0:T(8,128)(2,1)} %get-tuple-element.23), channel_id=1, source_target_pairs={{0,12},{12,0},{1,13},{13,1},{2,14},{14,2},{3,15},{15,3},{4,16},{16... | collective-permute-start | bytes 2654216 | tf_op jit(solution)/shard_map/ppermute | solution.py:164
  16.9 0.1 reshape.44
  17.0 39.1 %all_gather.9.own_ref = bf16[288,1536]{1,0:T(8,128)(2,1)S(1)} all-gather(bf16[24,1536]{1,0:T(8,128)(2,1)S(1)} %reshape.44), channel_id=1, replica_groups=mesh['xh'=2,'y'=8,'c'=2,'xl'=2,'z'=12] {'z'}, dimensions={0}, use_global_device_ids=true | all-gather | bytes 958464 | tf_op jit(solution)/shard_map/all_gather | solution.py:172
  56.1 3.2 %collective-permute-start = (bf16[288,1536]{1,0:T(8,128)(2,1)S(1)}, bf16[288,1536]{1,0:T(8,128)(2,1)S(1)}, u32[]{:S(2)}, u32[]{:S(2)}) collective-permute-start(bf16[288,1536]{1,0:T(8,128)(2,1)S(1)} %all_gather.9.own_ref), channel_id=1, source_target_pairs={{0,12},{12,0},{1,13},{13,1},{2,14},{14,2},{3,15},{15,3},{4,16},{16... | collective-permute-start | bytes 2654216 | tf_op jit(solution)/shard_map/ppermute | solution.py:164
  59.3 0.7 shard_map.76
  60.0 11.4 %all_to_all.10 = f32[8,48,128]{2,1,0:T(8,128)S(1)} all-to-all(f32[8,48,128]{2,1,0:T(8,128)S(1)} %shard_map.76), channel_id=1, replica_groups=mesh['xh'=2,'y'=8,'c'=2,'xl'=2,'z'=12] {'y'}, dimensions={0} | all-to-all | bytes 393216 | tf_op jit(solution)/shard_map/all_to_all | solution.py:160
  71.4 4.7 %collective-permute-done.other_ref = bf16[288,1536]{1,0:T(8,128)(2,1)S(1)} collective-permute-done((bf16[288,1536]{1,0:T(8,128)(2,1)S(1)}, bf16[288,1536]{1,0:T(8,128)(2,1)S(1)}, u32[]{:S(2)}, u32[]{:S(2)}) %collective-permute-start) | collective-permute-done | bytes 884768 | tf_op jit(solution)/shard_map/ppermute | solution.py:164
  76.1 0.9 copy-done.1
  77.0 0.7 copy-done.2
  77.7 2.8 %shard_map.77 = (bf16[144,6144]{1,0:T(8,128)(2,1)S(1)}, bf16[16,192,256]{2,1,0:T(8,128)(2,1)S(1)}, bf16[16,192,256]{2,1,0:T(8,128)(2,1)S(1)}) custom-call(bf16[288,1536]{1,0:T(8,128)(2,1)S(1)} %all_gather.9.own_ref, bf16[288,1536]{1,0:T(8,128)(2,1)S(1)} %collective-permute-done.other_ref, bf16[144,256]{1,0:T(8,128)(2,1)S(1)} %copy-done.1, f32[1,6144]{1,0:T(1,128)S(1)} %bitcast.7), custom_call_target="tpu_custom_call" | custom-call | flops 452984832 | bytes 10485760 | tf_op jit(solution)/shard_map/pallas_call | solution.py:143
  80.5 1.9 %collective-permute-start.2 = (bf16[16,192,256]{2,1,0:T(8,128)(2,1)S(1)}, bf16[16,192,256]{2,1,0:T(8,128)(2,1)S(1)}, u32[]{:S(2)}, u32[]{:S(2)}) collective-permute-start(bf16[16,192,256]{2,1,0:T(8,128)(2,1)S(1)} %get-tuple-element.26), channel_id=1, source_target_pairs={{0,24},{24,0},{1,25},{25,1},{2,26},{26,2},{3,27},{27,3},{4,28},{28... | collective-permute-start | bytes 4718600 | tf_op jit(solution)/shard_map/ppermute | solution.py:164
  82.5 2.0 %collective-permute-start.3 = (f32[48,128]{1,0:T(8,128)S(1)}, f32[48,128]{1,0:T(8,128)S(1)}, u32[]{:S(2)}, u32[]{:S(2)}) collective-permute-start(f32[48,128]{1,0:T(8,128)S(1)} %reduce_sum.45), channel_id=1, source_target_pairs={{0,384},{384,0},{1,385},{385,1},{2,386},{386,2},{3,387},{387,3},{4... | collective-permute-start | bytes 73736 | tf_op jit(solution)/shard_map/ppermute | solution.py:164
  84.5 3.2 %convolution_convert_fusion = bf16[144,256]{1,0:T(8,128)(2,1)} fusion(bf16[144,6144]{1,0:T(8,128)(2,1)S(1)} %get-tuple-element.28, bf16[6144,256]{1,0:T(8,128)(2,1)} %param.6), kind=kOutput, calls=%fused_computation.1 | convolution fusion | flops 453021696 | bytes 4988928 | tf_op jit(solution)/shard_map/dot_general | solution.py:181
  87.6 2.1 %collective-permute-done.3 = f32[48,128]{1,0:T(8,128)S(1)} collective-permute-done((f32[48,128]{1,0:T(8,128)S(1)}, f32[48,128]{1,0:T(8,128)S(1)}, u32[]{:S(2)}, u32[]{:S(2)}) %collective-permute-start.3) | collective-permute-done | bytes 24608 | tf_op jit(solution)/shard_map/ppermute | solution.py:164
  89.7 1.7 %add.25 = bf16[16,192,256]{2,1,0:T(8,128)(2,1)} add(bf16[16,192,256]{2,1,0:T(8,128)(2,1)S(1)} %get-tuple-element.25, bf16[16,192,256]{2,1,0:T(8,128)(2,1)S(1)} %collective-permute-done.2) | non-fusion elementwise | flops 786432 | bytes 4718592 | tf_op jit(solution)/shard_map/add | solution.py:180
  91.4 9.2 %all-to-all-start.1 = ((bf16[16,192,256]{2,1,0:T(8,128)(2,1)}), bf16[16,192,256]{2,1,0:T(8,128)(2,1)S(1)}, u32[]{:S(2)}, u32[]{:S(2)}) async-start(bf16[16,192,256]{2,1,0:T(8,128)(2,1)} %add.25), calls=%async_computation.2 | async-start | bytes 3145728 | tf_op jit(solution)/shard_map/all_to_all | solution.py:160
  100.6 0.2 fusion.6
  100.8 21.2 %all-gather = f32[576,128]{1,0:T(8,128)S(1)} all-gather(f32[48,128]{1,0:T(8,128)S(1)} %add.26), channel_id=2, replica_groups=mesh['xh'=2,'y'=8,'c'=2,'xl'=2,'z'=12] {'z'}, dimensions={0}, use_global_device_ids=true | all-gather | bytes 319488 | tf_op jit(solution)/shard_map/all_gather | solution.py:187
  122.0 3.6 %collective-permute-start.5 = (f32[48,128]{1,0:T(8,128)S(1)}, f32[48,128]{1,0:T(8,128)S(1)}, u32[]{:S(2)}, u32[]{:S(2)}) collective-permute-start(f32[48,128]{1,0:T(8,128)S(1)} %reduce_sum.47), channel_id=1, source_target_pairs={{0,12},{12,0},{1,13},{13,1},{2,14},{14,2},{3,15},{15,3},{4,16},{16... | collective-permute-start | bytes 73736 | tf_op jit(solution)/shard_map/ppermute | solution.py:164
  125.6 6.0 %collective-permute-done.5 = f32[48,128]{1,0:T(8,128)S(1)} collective-permute-done((f32[48,128]{1,0:T(8,128)S(1)}, f32[48,128]{1,0:T(8,128)S(1)}, u32[]{:S(2)}, u32[]{:S(2)}) %collective-permute-start.5) | collective-permute-done | bytes 24608 | tf_op jit(solution)/shard_map/ppermute | solution.py:164
  131.5 1.9 %collective-permute-start.6 = (f32[48,128]{1,0:T(8,128)S(1)}, f32[48,128]{1,0:T(8,128)S(1)}, u32[]{:S(2)}, u32[]{:S(2)}) collective-permute-start(f32[48,128]{1,0:T(8,128)S(1)} %add.29), channel_id=1, source_target_pairs={{0,24},{24,0},{1,25},{25,1},{2,26},{26,2},{3,27},{27,3},{4,28},{28... | collective-permute-start | bytes 73736 | tf_op jit(solution)/shard_map/ppermute | solution.py:164
  133.5 0.1 select_n.19
  133.5 2.3 %collective-permute-start.4 = (bf16[6,6144]{1,0:T(8,128)(2,1)S(1)}, bf16[6,6144]{1,0:T(8,128)(2,1)S(1)}, u32[]{:S(2)}, u32[]{:S(2)}) collective-permute-start(bf16[6,6144]{1,0:T(8,128)(2,1)S(1)} %select_n.19), channel_id=1, source_target_pairs={{0,12},{12,0},{1,13},{13,1},{2,14},{14,2},{3,15},{15,3},{4,16},{16... | collective-permute-start | bytes 221192 | tf_op jit(solution)/shard_map/ppermute | solution.py:164
  135.8 0.1 reshape.48
  135.9 0.6 add_bitcast_fusion
  136.5 4.1 %collective-permute-done.4 = bf16[6,6144]{1,0:T(8,128)(2,1)S(1)} collective-permute-done((bf16[6,6144]{1,0:T(8,128)(2,1)S(1)}, bf16[6,6144]{1,0:T(8,128)(2,1)S(1)}, u32[]{:S(2)}, u32[]{:S(2)}) %collective-permute-start.4) | collective-permute-done | bytes 73760 | tf_op jit(solution)/shard_map/ppermute | solution.py:164
  140.6 0.2 fusion.2
  140.9 0.7 fusion.5
  141.6 0.9 convert_reduce_fusion
  (24 shorter events, 0.1 us)
Async XLA Ops:
  7.2 84.2 %reduce-scatter.2.cloned.1.call-start = ((), (), s32[]{:S(2)}) async-start(), calls=%async_computation.3 | async-start | bytes 1916928 | tf_op jit(solution)/shard_map/reduce_scatter | solution.py:169
  7.2 9.7 %copy-start.4 = (bf16[6,6144]{1,0:T(8,128)(2,1)S(1)}, bf16[6,6144]{1,0:T(8,128)(2,1)}, u32[]{:S(2)}) copy-start(bf16[6,6144]{1,0:T(8,128)(2,1)} %param.4) | copy-start | bytes 221188
  13.7 45.6 %copy-start = (bf16[288,1536]{1,0:T(8,128)(2,1)S(1)}, bf16[288,1536]{1,0:T(8,128)(2,1)}, u32[]{:S(2)}) copy-start(bf16[288,1536]{1,0:T(8,128)(2,1)} %get-tuple-element.22.keep_ref) | copy-start | bytes 2654212
  13.7 45.6 %collective-permute-start.1 = (bf16[288,1536]{1,0:T(8,128)(2,1)}, bf16[288,1536]{1,0:T(8,128)(2,1)S(1)}, u32[]{:S(2)}, u32[]{:S(2)}) collective-permute-start(bf16[288,1536]{1,0:T(8,128)(2,1)} %get-tuple-element.23), channel_id=1, source_target_pairs={{0,12},{12,0},{1,13},{13,1},{2,14},{14,2},{3,15},{15,3},{4,16},{16... | collective-permute-start | bytes 2654216 | tf_op jit(solution)/shard_map/ppermute | solution.py:164
  56.1 20.0 %collective-permute-start = (bf16[288,1536]{1,0:T(8,128)(2,1)S(1)}, bf16[288,1536]{1,0:T(8,128)(2,1)S(1)}, u32[]{:S(2)}, u32[]{:S(2)}) collective-permute-start(bf16[288,1536]{1,0:T(8,128)(2,1)S(1)} %all_gather.9.own_ref), channel_id=1, source_target_pairs={{0,12},{12,0},{1,13},{13,1},{2,14},{14,2},{3,15},{15,3},{4,16},{16... | collective-permute-start | bytes 2654216 | tf_op jit(solution)/shard_map/ppermute | solution.py:164
  76.1 0.9 copy-start.1
  77.0 0.7 copy-start.2
  80.5 9.2 %collective-permute-start.2 = (bf16[16,192,256]{2,1,0:T(8,128)(2,1)S(1)}, bf16[16,192,256]{2,1,0:T(8,128)(2,1)S(1)}, u32[]{:S(2)}, u32[]{:S(2)}) collective-permute-start(bf16[16,192,256]{2,1,0:T(8,128)(2,1)S(1)} %get-tuple-element.26), channel_id=1, source_target_pairs={{0,24},{24,0},{1,25},{25,1},{2,26},{26,2},{3,27},{27,3},{4,28},{28... | collective-permute-start | bytes 4718600 | tf_op jit(solution)/shard_map/ppermute | solution.py:164
  82.5 7.2 %collective-permute-start.3 = (f32[48,128]{1,0:T(8,128)S(1)}, f32[48,128]{1,0:T(8,128)S(1)}, u32[]{:S(2)}, u32[]{:S(2)}) collective-permute-start(f32[48,128]{1,0:T(8,128)S(1)} %reduce_sum.45), channel_id=1, source_target_pairs={{0,384},{384,0},{1,385},{385,1},{2,386},{386,2},{3,387},{387,3},{4... | collective-permute-start | bytes 73736 | tf_op jit(solution)/shard_map/ppermute | solution.py:164
  91.4 9.3 %copy-start.5 = (bf16[6,6144]{1,0:T(8,128)(2,1)S(1)}, bf16[6,6144]{1,0:T(8,128)(2,1)}, u32[]{:S(2)}) copy-start(bf16[6,6144]{1,0:T(8,128)(2,1)} %param.4) | copy-start | bytes 221188
  91.4 49.3 %copy-start.3 = (f32[6144]{0:T(1024)S(1)}, f32[6144]{0:T(1024)}, u32[]{:S(2)}) copy-start(f32[6144]{0:T(1024)} %param.5) | copy-start | bytes 73732
  91.4 42.1 %copy-start.6 = (bf16[48,1536]{1,0:T(8,128)(2,1)S(1)}, bf16[48,1536]{1,0:T(8,128)(2,1)}, u32[]{:S(2)}) copy-start(bf16[48,1536]{1,0:T(8,128)(2,1)} %reduce-scatter.2.cloned.1.call-done) | copy-start | bytes 442372
  91.4 50.3 %all-to-all-start.1 = ((bf16[16,192,256]{2,1,0:T(8,128)(2,1)}), bf16[16,192,256]{2,1,0:T(8,128)(2,1)S(1)}, u32[]{:S(2)}, u32[]{:S(2)}) async-start(bf16[16,192,256]{2,1,0:T(8,128)(2,1)} %add.25), calls=%async_computation.2 | async-start | bytes 3145728 | tf_op jit(solution)/shard_map/all_to_all | solution.py:160
  122.0 9.5 %collective-permute-start.5 = (f32[48,128]{1,0:T(8,128)S(1)}, f32[48,128]{1,0:T(8,128)S(1)}, u32[]{:S(2)}, u32[]{:S(2)}) collective-permute-start(f32[48,128]{1,0:T(8,128)S(1)} %reduce_sum.47), channel_id=1, source_target_pairs={{0,12},{12,0},{1,13},{13,1},{2,14},{14,2},{3,15},{15,3},{4,16},{16... | collective-permute-start | bytes 73736 | tf_op jit(solution)/shard_map/ppermute | solution.py:164
  131.5 4.4 %collective-permute-start.6 = (f32[48,128]{1,0:T(8,128)S(1)}, f32[48,128]{1,0:T(8,128)S(1)}, u32[]{:S(2)}, u32[]{:S(2)}) collective-permute-start(f32[48,128]{1,0:T(8,128)S(1)} %add.29), channel_id=1, source_target_pairs={{0,24},{24,0},{1,25},{25,1},{2,26},{26,2},{3,27},{27,3},{4,28},{28... | collective-permute-start | bytes 73736 | tf_op jit(solution)/shard_map/ppermute | solution.py:164
  133.5 7.1 %collective-permute-start.4 = (bf16[6,6144]{1,0:T(8,128)(2,1)S(1)}, bf16[6,6144]{1,0:T(8,128)(2,1)S(1)}, u32[]{:S(2)}, u32[]{:S(2)}) collective-permute-start(bf16[6,6144]{1,0:T(8,128)(2,1)S(1)} %select_n.19), channel_id=1, source_target_pairs={{0,12},{12,0},{1,13},{13,1},{2,14},{14,2},{3,15},{15,3},{4,16},{16... | collective-permute-start | bytes 221192 | tf_op jit(solution)/shard_map/ppermute | solution.py:164
Sparse Core Ops, SparseCore 0:
  13.8 68.0 reduce-scatter.1
